TPU v7x, 32 devices: a whole 2x2x4 slice. The times are simulated.
32 devices in a mesh: row: 8 (over z, core), col: 4 (over y, x).
Axes of the slice: x: 2, y: 2, z: 4, core: 2. Of those that a mesh axis runs over, the one named last changes fastest.
Arguments:
- object_field: float32 [2, 2048, 1024], P(None, 'row', 'col'), may hold values from -1.8 to 1.8
- probe: float32 [2, 256, 256], replicated, may hold values from -0.4 to 0.4
- coeffs: float32 [3, 256, 256], replicated, may hold values from 0.5 to 1.5
- patterns: float32 [8, 4, 4, 256, 256], P('row', 'col'), may hold values from 0 to 1
- offsets: int32 [8, 4, 4, 2], P('row', 'col'), may hold values from 0 to 255
Outputs:
- object_out: float32 [2, 2048, 1024], P(None, 'row', 'col')
- coeffs_out: float32 [3, 256, 256], replicated
All inputs are finite; a program needn't handle non-finite values.
Results may differ from a plain program's by a relative error of at most 0.0003.
Values sent between devices are 32-bit elements; how exact they have to be, the bound alone decides.
A program may use at most 64 MiB of HBM per device.

v0:
```python
import functools

import jax
import jax.numpy as jnp
import ml_dtypes
import numpy as np
from jax import lax
from jax.experimental import pallas as pl
from jax.experimental.pallas import tpu as pltpu
from jax.sharding import PartitionSpec as P

ITERS = 2


STEP_RATE = 0.2
RIDGE = 1.0
EPSILON = 1e-06


def dft_stacks(order):
    index = np.arange(order)
    angle = -2.0 * np.pi / order * (index[:, None] * index[None, :] % order)
    real, imag = np.cos(angle) / np.sqrt(order), np.sin(angle) / np.sqrt(order)
    left = np.block([[real, -imag], [imag, real]]).astype(np.float32)
    stacks = []
    for full in (left, left.T):
        high = full.astype(ml_dtypes.bfloat16)
        low = (full - high.astype(np.float32)).astype(ml_dtypes.bfloat16)
        stacks += [high, low]
    return [jnp.asarray(stack) for stack in stacks]


def dot(left, right):
    return jnp.dot(left, right, preferred_element_type=jnp.float32)


def split(full):
    high = full.astype(jnp.bfloat16)
    return high, (full - high.astype(jnp.float32)).astype(jnp.bfloat16)


def transform(real, imag, left_high, left_low, right_high, right_low):
    width = real.shape[0]
    high, low = split(jnp.concatenate([real, imag], axis=0))
    rows = dot(left_high, high) + dot(left_high, low) + dot(left_low, high)
    high, low = split(jnp.concatenate([rows[:width], rows[width:]], axis=1))
    cols = dot(high, right_high) + dot(low, right_high) + dot(high, right_low)
    return cols[:, :width], cols[:, width:]


def visit_kernel(offs, ext, probe, coeffs, pats, ah, al, bh, bl, grad, stats):
    width = probe.shape[1]
    size = ext.shape[1]
    tile = size - width
    grad[...] = jnp.zeros_like(grad)
    stats[...] = jnp.zeros_like(stats)

    def visit(p, carry):
        oy, ox = offs[p, 0], offs[p, 1]
        odd = lax.rem(oy, 8)
        even = pl.multiple_of(oy - odd, 8)
        window = []
        for part in (0, 1):
            rows = pltpu.roll(ext[part, pl.ds(even, width + 8), :], lax.rem(size - ox, size), axis=1)
            rows = pltpu.roll(rows[:, :width], lax.rem(width + 8 - odd, width + 8), axis=0)
            window.append(rows[:width])
        pr, pi = probe[0], probe[1]
        wr, wi = transform(
            pr * window[0] - pi * window[1],
            pr * window[1] + pi * window[0],
            ah[...], al[...], bh[...], bl[...],
        )
        inten = wr * wr + wi * wi
        lin, quad, cubic = coeffs[0], coeffs[1], coeffs[2]
        error = inten * (lin + inten * (quad + inten * cubic)) - pats[p]
        weight = 2.0 * error * (lin + inten * (2.0 * quad + 3.0 * cubic * inten))
        squared = inten * inten
        cubed = squared * inten
        stats[0] += error * inten
        stats[1] += error * squared
        stats[2] += error * cubed
        stats[3] += squared
        stats[4] += squared * squared
        stats[5] += cubed * cubed
        br, bi = transform(weight * wr, weight * wi, bh[...], bl[...], ah[...], al[...])
        below = jnp.zeros((8, width), jnp.float32)
        beside = jnp.zeros((width + 8, tile), jnp.float32)
        for part, g in ((0, pr * br + pi * bi), (1, pr * bi - pi * br)):
            g = pltpu.roll(jnp.concatenate([g, below], axis=0), odd, axis=0)
            g = pltpu.roll(jnp.concatenate([g, beside], axis=1), ox, axis=1)
            grad[part, pl.ds(even, width + 8), :] += g
        return carry

    lax.fori_loop(0, pats.shape[0], visit, 0, unroll=True)


def visit_windows(offs, ext, probe, coeffs, pats, stacks):
    width = probe.shape[1]
    size = ext.shape[1]
    vmem = pl.BlockSpec(memory_space=pltpu.VMEM)
    return pl.pallas_call(
        visit_kernel,
        out_shape=(
            jax.ShapeDtypeStruct(ext.shape, jnp.float32),
            jax.ShapeDtypeStruct((6, width, width), jnp.float32),
        ),
        in_specs=[pl.BlockSpec(memory_space=pltpu.SMEM)] + [vmem] * 8,
        out_specs=(vmem, vmem),
        compiler_params=pltpu.CompilerParams(vmem_limit_bytes=40 * 1024 * 1024),
        name="visit_windows",
    )(offs, ext, probe, coeffs, pats, *stacks)


class Link:
    def __init__(self, axis, step, source, target, sems, slot):
        self.axis, self.step = axis, step
        here, count = lax.axis_index(axis), lax.axis_size(axis)
        self.copy = remote(
            source, target, sems, slot, {axis: lax.rem(here + step + count, count)}
        )

    def exists(self, step):
        here, count = lax.axis_index(self.axis), lax.axis_size(self.axis)
        return here > 0 if step < 0 else here < count - 1

    def start(self):
        pl.when(self.exists(self.step))(self.copy.start)
        return self

    def arrived(self, then=None):
        @pl.when(self.exists(-self.step))
        def _():
            self.copy.wait_recv()
            if then is not None:
                then()

    def sent(self):
        pl.when(self.exists(self.step))(self.copy.wait_send)


def remote(source, target, sems, slot, device):
    send, recv = sems
    where = tuple(device.get(axis, lax.axis_index(axis)) for axis in ("row", "col"))
    return pltpu.make_async_remote_copy(
        src_ref=source,
        dst_ref=target,
        send_sem=send.at[slot],
        recv_sem=recv.at[slot],
        device_id=where,
        device_id_type=pl.DeviceIdType.MESH,
    )


def greet():
    barrier = pltpu.get_barrier_semaphore()
    count = 0
    for axis in ("row", "col"):
        size = lax.axis_size(axis)
        here = lax.axis_index(axis)
        for distance in range(1, size):
            other = {"row": lax.axis_index("row"), "col": lax.axis_index("col")}
            other[axis] = lax.rem(here + distance, size)
            pl.semaphore_signal(
                barrier,
                inc=1,
                device_id=(other["row"], other["col"]),
                device_id_type=pl.DeviceIdType.MESH,
            )
            count += 1
    pl.semaphore_wait(barrier, count)


class Slots:
    def __init__(self, sems):
        self.sems, self.used = sems, 0

    def next(self):
        self.used += 1
        return self.used - 1


def copies_needed():
    rows, cols = lax.axis_size("row"), lax.axis_size("col")
    return 2 * (1 + cols + rows // 2) + cols + rows + 16


def halo_cols(field, part, half, tile, slots):
    inner = pl.ds(half, tile)
    return [
        Link("col", -1, field.at[part, inner, half : 2 * half],
             field.at[part, inner, half + tile :], slots.sems, slots.next()).start(),
        Link("col", 1, field.at[part, inner, tile : half + tile],
             field.at[part, inner, :half], slots.sems, slots.next()).start(),
    ]


def halo_rows(field, part, half, tile, slots):
    return [
        Link("row", -1, field.at[part, half : 2 * half, :],
             field.at[part, half + tile :, :], slots.sems, slots.next()).start(),
        Link("row", 1, field.at[part, tile : half + tile, :],
             field.at[part, :half, :], slots.sems, slots.next()).start(),
    ]


def fold_rows(grad, into, part, half, tile, slots):
    return [
        Link("row", -1, grad.at[part, :half, :], into.at[0, part], slots.sems, slots.next()).start(),
        Link("row", 1, grad.at[part, half + tile :, :], into.at[1, part], slots.sems, slots.next()).start(),
    ]


def fold_cols(mid, into, part, half, tile, slots):
    return [
        Link("col", -1, mid.at[part, :, :half], into.at[0, part], slots.sems, slots.next()).start(),
        Link("col", 1, mid.at[part, :, half + tile :], into.at[1, part], slots.sems, slots.next()).start(),
    ]


def update_kernel(last, grad, stats, field, coeffs, field_out, coeffs_out,
                  gfull, from_rows, mid, from_cols, half_sums, col_sums, shard, z_sums,
                  new_coeffs, sq_mine, sq_cols, sq_part, sq_rows, send_sem, recv_sem):
    rows, cols = lax.axis_size("row"), lax.axis_size("col")
    r, c = lax.axis_index("row"), lax.axis_index("col")
    depth = rows // 2
    k, z = lax.rem(r, 2), lax.div(r, 2)
    width = stats.shape[1]
    half = width // 2
    tile = grad.shape[1] - width
    slots = Slots((send_sem, recv_sem))
    rows1, rows2, rows3 = half_sums.shape[1], shard.shape[1], z_sums.shape[2]
    cut = rows3 < rows2

    gfull[...] = jnp.zeros_like(gfull)
    greet()

    def at(start, size):
        return pl.ds(pl.multiple_of(start, 8), size)

    def to(source, target, device):
        copy = remote(source, target, slots.sems, slots.next(), device)
        copy.start()
        return copy

    links = []

    def send(start, *refs):
        pair = start(*refs, half, tile, slots)
        links.extend(pair)
        return pair

    row_links = [send(fold_rows, grad, from_rows, part) for part in (0, 1)]
    partner = {"row": r + 1 - 2 * k}
    pair = to(stats.at[:, at((1 - k) * rows1, rows1), :], half_sums, partner)
    mid[...] = grad[:, half : half + tile, :]

    pair.wait_recv()
    half_sums[...] += stats[:, at(k * rows1, rows1), :]
    over_cols = []
    for d in range(1, cols):
        other = lax.rem(c + d, cols)
        over_cols.append(
            to(half_sums.at[:, at(other * rows2, rows2), :], col_sums.at[d - 1], {"col": other})
        )

    col_links = []
    for part in (0, 1):
        def add_low():
            mid[part, tile - half :, :] += from_rows[0, part]

        def add_high():
            mid[part, :half, :] += from_rows[1, part]

        row_links[part][0].arrived(add_low)
        row_links[part][1].arrived(add_high)
        col_links.append(send(fold_cols, mid, from_cols, part))

    for copy in over_cols:
        copy.wait_recv()
    shard[...] = half_sums[:, at(c * rows2, rows2), :] + sum(col_sums[d] for d in range(cols - 1))
    over_z = []
    for d in range(1, depth):
        other = lax.rem(z + d, depth)
        source = shard.at[:, at(other * rows3, rows3), :] if cut else shard
        over_z.append(to(source, z_sums.at[z], {"row": 2 * other + k}))
    z_sums[z] = shard[:, at(z * rows3, rows3), :] if cut else shard[...]

    inner = pl.ds(half, tile)
    side_links = []
    square = 0.0
    for part in (0, 1):
        gfull[part, inner, half : half + tile] = mid[part, :, half : half + tile]

        def add_low():
            gfull[part, inner, tile : half + tile] += from_cols[0, part]

        def add_high():
            gfull[part, inner, half : 2 * half] += from_cols[1, part]

        col_links[part][0].arrived(add_low)
        col_links[part][1].arrived(add_high)
        if not last:
            side_links.append(send(halo_cols, gfull, part))
        mine = gfull[part, inner, half : half + tile]
        square += jnp.sum((mine * mine).reshape(-1, 8, tile), axis=0)
    sq_mine[...] = sum(square[:, i : i + 128] for i in range(0, tile, 128))
    sq_over_cols = [
        to(sq_mine, sq_cols.at[d - 1], {"col": lax.rem(c + d, cols)}) for d in range(1, cols)
    ]

    for copy in over_z:
        copy.wait_recv()
    sums = sum(z_sums[i] for i in range(depth))
    base2 = k * rows1 + c * rows2
    base3 = base2 + z * rows3 if cut else base2
    new_coeffs[:, at(base3, rows3), :] = coeffs[:, at(base3, rows3), :] - sums[:3] / (sums[3:] + RIDGE)
    back = []
    if cut:
        ready = new_coeffs.at[:, at(base3, rows3), :]
        for d in range(1, depth):
            back.append(to(ready, ready, {"row": 2 * lax.rem(z + d, depth) + k}))

    for copy in sq_over_cols:
        copy.wait_recv()
    sq_part[...] = sq_mine[...] + sum(sq_cols[d] for d in range(cols - 1))
    sq_over_rows = [
        to(sq_part, sq_rows.at[d - 1], {"row": lax.rem(r + d, rows)}) for d in range(1, rows)
    ]

    end_links = []
    if not last:
        for part in (0, 1):
            for link in side_links[part]:
                link.arrived()
            end_links.append(send(halo_rows, gfull, part))
    for copy in back:
        copy.wait_recv()
    ready = new_coeffs.at[:, at(base2, rows2), :]
    wide = [to(ready, ready, {"col": lax.rem(c + d, cols)}) for d in range(1, cols)]

    for copy in sq_over_rows:
        copy.wait_recv()
    square = sq_part[...] + sum(sq_rows[d] for d in range(rows - 1))
    total = 2.0 * tile * tile * rows * cols
    rate = STEP_RATE / jnp.sqrt(jnp.sum(square, keepdims=True) / total + EPSILON)
    if last:
        for part in (0, 1):
            field_out[part] = field[part, inner, half : half + tile] - rate * gfull[part, inner, half : half + tile]

    for copy in wide:
        copy.wait_recv()
    ready = new_coeffs.at[:, at(k * rows1, rows1), :]
    final = to(ready, ready, partner)
    if not last:
        for part in (0, 1):
            for link in end_links[part]:
                link.arrived()
            field_out[part] = field[part] - rate * gfull[part]
    final.wait_recv()
    coeffs_out[...] = new_coeffs[...]
    for link in links:
        link.sent()
    for copy in [pair, final] + over_cols + sq_over_cols + sq_over_rows + over_z + back + wide:
        copy.wait_send()


def update(last, grad, stats, field, coeffs):
    rows, cols = lax.axis_size("row"), lax.axis_size("col")
    depth = rows // 2
    size, width = grad.shape[1], stats.shape[1]
    half, tile = width // 2, size - width
    rows1 = width // 2
    rows2 = rows1 // cols
    rows3 = rows2 // depth if rows2 % (8 * depth) == 0 else rows2
    vmem = pl.BlockSpec(memory_space=pltpu.VMEM)
    f32 = jnp.float32
    count = copies_needed()
    side = tile if last else size
    return pl.pallas_call(
        functools.partial(update_kernel, last),
        out_shape=(
            jax.ShapeDtypeStruct((2, side, side), f32),
            jax.ShapeDtypeStruct(coeffs.shape, f32),
        ),
        in_specs=[vmem] * 4,
        out_specs=(vmem, vmem),
        scratch_shapes=[
            pltpu.VMEM((2, size, size), f32),
            pltpu.VMEM((2, 2, half, size), f32),
            pltpu.VMEM((2, tile, size), f32),
            pltpu.VMEM((2, 2, tile, half), f32),
            pltpu.VMEM((6, rows1, width), f32),
            pltpu.VMEM((cols - 1, 6, rows2, width), f32),
            pltpu.VMEM((6, rows2, width), f32),
            pltpu.VMEM((depth, 6, rows3, width), f32),
            pltpu.VMEM(coeffs.shape, f32),
            pltpu.VMEM((8, 128), f32),
            pltpu.VMEM((cols - 1, 8, 128), f32),
            pltpu.VMEM((8, 128), f32),
            pltpu.VMEM((rows - 1, 8, 128), f32),
            pltpu.SemaphoreType.DMA((count,)),
            pltpu.SemaphoreType.DMA((count,)),
        ],
        compiler_params=pltpu.CompilerParams(
            collective_id=2 if last else 1,
            has_side_effects=True,
            vmem_limit_bytes=48 * 1024 * 1024,
        ),
        name="update_last" if last else "update",
    )(grad, stats, field, coeffs)


def extend_kernel(half, tile, field, out, full, send, recv):
    full[...] = jnp.zeros_like(full)
    inner = pl.ds(half, tile)
    full[:, inner, half : half + tile] = field[...]
    barrier = pltpu.get_barrier_semaphore()
    count = jnp.int32(0)
    for axis in ("row", "col"):
        size = lax.axis_size(axis)
        here = lax.axis_index(axis)
        for step in (-1, 1):
            other = {"row": lax.axis_index("row"), "col": lax.axis_index("col")}
            other[axis] = lax.rem(here + step + size, size)
            exists = here > 0 if step < 0 else here < size - 1
            count += exists.astype(jnp.int32)

            @pl.when(exists)
            def _():
                pl.semaphore_signal(
                    barrier,
                    inc=1,
                    device_id=(other["row"], other["col"]),
                    device_id_type=pl.DeviceIdType.MESH,
                )

    pl.semaphore_wait(barrier, count)
    slots = Slots((send, recv))
    side = [halo_cols(full, part, half, tile, slots) for part in (0, 1)]
    ends = []
    for part in (0, 1):
        for link in side[part]:
            link.arrived()
        ends.append(halo_rows(full, part, half, tile, slots))
    for part in (0, 1):
        for link in ends[part]:
            link.arrived()
    out[...] = full[...]
    for links in side + ends:
        for link in links:
            link.sent()


def extend(field, half):
    tile = field.shape[1]
    size = tile + 2 * half
    vmem = pl.BlockSpec(memory_space=pltpu.VMEM)
    return pl.pallas_call(
        functools.partial(extend_kernel, half, tile),
        out_shape=jax.ShapeDtypeStruct((2, size, size), jnp.float32),
        in_specs=[vmem],
        out_specs=vmem,
        scratch_shapes=[
            pltpu.VMEM((2, size, size), jnp.float32),
            pltpu.SemaphoreType.DMA((8,)),
            pltpu.SemaphoreType.DMA((8,)),
        ],
        compiler_params=pltpu.CompilerParams(
            collective_id=0, has_side_effects=True, vmem_limit_bytes=32 * 1024 * 1024
        ),
        name="extend",
    )(field)


def local(object_field, probe, coeffs, patterns, offsets):
    width = probe.shape[1]
    stacks = dft_stacks(width)
    flat_pats = patterns.reshape(-1, width, width)
    flat_offs = offsets.reshape(-1, 2)
    field = extend(object_field, width // 2)
    for turn in range(ITERS):
        grad, stats = visit_windows(flat_offs, field, probe, coeffs, flat_pats, stacks)
        field, coeffs = update(turn == ITERS - 1, grad, stats, field, coeffs)
    return (field, coeffs)


def solution(mesh):
    placed = (
        P(None, "row", "col"),
        P(),
        P(),
        P("row", "col", None, None, None),
        P("row", "col", None, None),
    )
    return jax.shard_map(
        local, mesh=mesh, in_specs=placed, out_specs=(P(None, "row", "col"), P()), check_vma=False
    )
```

profile of v0, /device:TPU:0, one launch (start us, length us, event | category | flops | bytes accessed | tf_op | source)
XLA Modules:
  0.0 150.2 jit_solution(6312183792350247752)
XLA Ops:
  0.6 0.0 copy-start.3
  0.6 0.0 copy-start.5
  0.7 0.0 copy-start.2
  0.7 0.9 copy.12.offs
  1.6 0.0 copy-start.14
  1.6 1.0 copy-done.14
  2.6 15.8 %extend.1.ext.field = f32[2,512,512]{2,1,0:T(8,128)S(1)} custom-call(f32[2,256,256]{2,1,0:T(8,128)S(1)} %copy-done.14), custom_call_target="tpu_custom_call" | custom-call | tf_op jit(solution)/shard_map/extend/pallas_call | solution.py:458
  18.4 0.0 copy-done.3
  18.4 0.0 copy-done.5
  18.4 0.0 copy-done.2
  18.4 0.0 copy-start.6
  18.4 1.0 copy-done.6
  19.5 0.0 copy-start.8
  19.5 1.0 copy-done.8
  20.5 0.0 copy-start.10
  20.5 1.0 copy-done.10
  21.6 0.0 copy-start.12
  21.6 1.0 copy-done.12
  22.6 0.0 copy-start
  22.6 14.4 %visit_windows.2 = (f32[2,512,512]{2,1,0:T(8,128)S(1)}, f32[6,256,256]{2,1,0:T(8,128)S(1)}) custom-call(s32[4,2]{1,0:T(4,128)S(1)} %copy.12.offs, f32[2,512,512]{2,1,0:T(8,128)S(1)} %extend.1.ext.field, f32[2,256,256]{2,1,0:T(8,128)S(1)} %copy-done.5, f32[3,256,256]{2,1,0:T(8,128)S(1)} %copy-done.3, f32[4,256,256]{2,1,0:T(8,128)S(1)} %bitcast.2, ...), custom_call_target="tpu_custom_call" | custom-call | tf_op jit(solution)/shard_map/visit_windows/pallas_call | solution.py:101
  37.1 0.0 copy-done
  37.1 0.0 copy-start.4
  37.1 1.3 copy-done.4
  38.4 0.0 copy-start.7
  38.4 0.0 copy-start.9
  38.4 0.0 copy-start.11
  38.4 0.0 copy-start.13
  38.4 56.0 %update.1 = (f32[2,512,512]{2,1,0:T(8,128)S(1)}, f32[3,256,256]{2,1,0:T(8,128)S(1)}) custom-call(f32[2,512,512]{2,1,0:T(8,128)} %copy-done.4, f32[6,256,256]{2,1,0:T(8,128)S(1)} %get-tuple-element.9.stats, f32[2,512,512]{2,1,0:T(8,128)} %copy-done, f32[3,256,256]{2,1,0:T(8,128)S(1)} %copy-done.3), custom_call_target="tpu_custom_call" | custom-call | tf_op jit(solution)/shard_map/update/pallas_call | solution.py:379
  94.4 0.0 copy-start.1
  94.5 0.0 copy-done.7
  94.5 0.0 copy-done.9
  94.5 0.0 copy-done.11
  94.5 0.0 copy-done.13
  94.5 14.1 %visit_windows.3 = (f32[2,512,512]{2,1,0:T(8,128)S(1)}, f32[6,256,256]{2,1,0:T(8,128)S(1)}) custom-call(s32[4,2]{1,0:T(4,128)S(1)} %copy.12.offs, f32[2,512,512]{2,1,0:T(8,128)S(1)} %get-tuple-element.10.ext.field, f32[2,256,256]{2,1,0:T(8,128)S(1)} %copy-done.5, f32[3,256,256]{2,1,0:T(8,128)S(1)} %get-tuple-element.11.coeffs, f32[4,256,256]{2,1,0:T(8,128)S(1)} %bitcast.3, ...), custom_call_target="tpu_custom_call" | custom-call | tf_op jit(solution)/shard_map/visit_windows/pallas_call | solution.py:101
  108.6 0.0 copy-done.1
  108.6 40.0 %update_last.1 = (f32[2,256,256]{2,1,0:T(8,128)S(1)}, f32[3,256,256]{2,1,0:T(8,128)S(1)}) custom-call(f32[2,512,512]{2,1,0:T(8,128)S(1)} %get-tuple-element.12.grad, f32[6,256,256]{2,1,0:T(8,128)S(1)} %get-tuple-element.13.stats, f32[2,512,512]{2,1,0:T(8,128)} %copy-done.1, f32[3,256,256]{2,1,0:T(8,128)S(1)} %get-tuple-element.11.coeffs), custom_call_target="tpu_custom_call" | custom-call | tf_op jit(solution)/shard_map/update_last/pallas_call | solution.py:379
  148.5 0.8 copy.15
  149.3 0.9 copy.16
Async XLA Ops:
  0.6 17.8 %copy-start.3 = (f32[3,256,256]{2,1,0:T(8,128)S(1)}, f32[3,256,256]{2,1,0:T(8,128)}, u32[]{:S(2)}) copy-start(f32[3,256,256]{2,1,0:T(8,128)} %coeffs.3) | copy-start | bytes 2359300
  0.6 17.8 %copy-start.5 = (f32[2,256,256]{2,1,0:T(8,128)S(1)}, f32[2,256,256]{2,1,0:T(8,128)}, u32[]{:S(2)}) copy-start(f32[2,256,256]{2,1,0:T(8,128)} %probe.3) | copy-start | bytes 1572868
  0.7 17.8 %copy-start.2 = (f32[1,1,4,256,256]{4,3,2,1,0:T(8,128)S(1)}, f32[1,1,4,256,256]{4,3,2,1,0:T(8,128)}, u32[]{:S(2)}) copy-start(f32[1,1,4,256,256]{4,3,2,1,0:T(8,128)} %param.12) | copy-start | bytes 3145732
  1.6 1.0 copy-start.14
  18.4 1.0 copy-start.6
  19.5 1.0 copy-start.8
  20.5 1.0 copy-start.10
  21.6 1.0 copy-start.12
  22.6 14.4 %copy-start = (f32[2,512,512]{2,1,0:T(8,128)}, f32[2,512,512]{2,1,0:T(8,128)S(1)}, u32[]{:S(2)}) copy-start(f32[2,512,512]{2,1,0:T(8,128)S(1)} %extend.1.ext.field) | copy-start | bytes 6291460
  37.1 1.3 copy-start.4
  38.4 56.1 %copy-start.7 = (bf16[512,512]{1,0:T(8,128)(2,1)S(1)}, bf16[512,512]{1,0:T(8,128)(2,1)}, u32[]{:S(2)}) copy-start(bf16[512,512]{1,0:T(8,128)(2,1)} %constant.11.clone.bl) | copy-start | bytes 1572868
  38.4 56.1 %copy-start.9 = (bf16[512,512]{1,0:T(8,128)(2,1)S(1)}, bf16[512,512]{1,0:T(8,128)(2,1)}, u32[]{:S(2)}) copy-start(bf16[512,512]{1,0:T(8,128)(2,1)} %constant.10.clone.bh) | copy-start | bytes 1572868
  38.4 56.1 %copy-start.11 = (bf16[512,512]{1,0:T(8,128)(2,1)S(1)}, bf16[512,512]{1,0:T(8,128)(2,1)}, u32[]{:S(2)}) copy-start(bf16[512,512]{1,0:T(8,128)(2,1)} %constant.9.clone.al) | copy-start | bytes 1572868
  38.4 56.1 %copy-start.13 = (bf16[512,512]{1,0:T(8,128)(2,1)S(1)}, bf16[512,512]{1,0:T(8,128)(2,1)}, u32[]{:S(2)}) copy-start(bf16[512,512]{1,0:T(8,128)(2,1)} %constant.8.clone.ah) | copy-start | bytes 1572868
  94.4 14.1 %copy-start.1 = (f32[2,512,512]{2,1,0:T(8,128)}, f32[2,512,512]{2,1,0:T(8,128)S(1)}, u32[]{:S(2)}) copy-start(f32[2,512,512]{2,1,0:T(8,128)S(1)} %get-tuple-element.10.ext.field) | copy-start | bytes 6291460
where the time goes:
time: 151 us; the launch traced here: 150 us
  Pallas kernels  140 us (93%)
  local copies, waits for them, and re-layouts  9.16 us (6%)
    pallas_call x2, Pallas kernels, update(): pl.pallas_call(functools.partial(update_kernel, last), out_shape=(jax.Sha...  96 us
    pallas_call x2, Pallas kernels, visit_windows(): pl.pallas_call(visit_kernel, out_shape=(jax.ShapeDtypeStruct(ext.shape, j...  28.5 us
    pallas_call x1, Pallas kernels, extend(): pl.pallas_call(functools.partial(extend_kernel, half, tile), out_shape=ja...  15.8 us
    unnamed x32, local copies, waits for them, and re-layouts  8.24 us

commit v1 on v0

v1 whole, which is shorter than its diff:
```python
import functools

import jax
import jax.numpy as jnp
import ml_dtypes
import numpy as np
from jax import lax
from jax.experimental import pallas as pl
from jax.experimental.pallas import tpu as pltpu
from jax.sharding import PartitionSpec as P

STEP_RATE = 0.2
RIDGE = 1.0
EPSILON = 1e-06
LANES = 128
CHUNK = 16
F32 = jnp.float32
BF16 = jnp.bfloat16


def dft_halves(order):
    half = order // 2
    index = np.arange(order)
    angle = -2.0 * np.pi / order * (index[:, None] * index[None, :] % order)
    real, imag = np.cos(angle) / np.sqrt(order), np.sin(angle) / np.sqrt(order)
    lefts, rights = [], []
    for parity in (0, 1):
        re, im = real[parity::2, :half], imag[parity::2, :half]
        full = np.block([[re, -im], [im, re]]).astype(np.float32)
        for into, forward in ((lefts, full), (rights, full.T)):
            high = forward.astype(ml_dtypes.bfloat16)
            low = (forward - high.astype(np.float32)).astype(ml_dtypes.bfloat16)
            into.append((high, low))
    wide = lambda pair: np.concatenate([pair[0], pair[0], pair[1]], axis=1)
    tall = lambda pair: np.concatenate([pair[0], pair[0], pair[1]], axis=0)
    on_left = [wide(m) for m in lefts] + [wide(m) for m in rights]
    on_right = [tall(m) for m in rights] + [tall(m) for m in lefts]
    order_of = np.concatenate([index[0::2], index[1::2]])
    perm = (order_of[:, None] == index[None, :]).astype(ml_dtypes.bfloat16)
    on_left.append(np.concatenate([perm] * 3, axis=1))
    on_right.append(np.concatenate([perm.T] * 3, axis=0))
    on_right.append(np.concatenate([perm] * 3, axis=0))
    return jnp.asarray(np.stack(on_left)), jnp.asarray(np.stack(on_right))


def dot(left, right):
    return jnp.dot(left, right, preferred_element_type=F32)


def split(full):
    high = full.astype(BF16)
    return high, (full - high.astype(F32)).astype(BF16)


def split3(full):
    high = full.astype(BF16)
    rest = full - high.astype(F32)
    mid = rest.astype(BF16)
    return high, mid, (rest - mid.astype(F32)).astype(BF16)


def from_left(matrix, full):
    high, low = split(full)
    return dot(matrix, jnp.concatenate([high, low, high], axis=0))


def from_right(full, matrix):
    high, low = split(full)
    return dot(jnp.concatenate([high, low, high], axis=1), matrix)


class Copies:
    def __init__(self, send, recv):
        self.send, self.recv, self.used, self.made = send, recv, 0, []

    def make(self, source, target, row=None, col=None, sends=None, gets=None):
        slot = self.used
        self.used += 1
        where = (lax.axis_index("row") if row is None else row, lax.axis_index("col") if col is None else col)
        copy = pltpu.make_async_remote_copy(
            src_ref=source, dst_ref=target, send_sem=self.send.at[slot], recv_sem=self.recv.at[slot],
            device_id=where, device_id_type=pl.DeviceIdType.MESH,
        )
        made = Copy(copy, sends, gets)
        self.made.append(made)
        return made

    def finish(self):
        for made in self.made:
            made.sent()


def when(condition, act):
    if condition is None:
        act()
    else:
        pl.when(condition)(act)


class Copy:
    def __init__(self, copy, sends, gets):
        self.copy, self.sends, self.gets = copy, sends, gets

    def start(self):
        when(self.sends, self.copy.start)
        return self

    def arrived(self):
        when(self.gets, self.copy.wait_recv)

    def sent(self):
        when(self.sends, self.copy.wait_send)


def both(a, b):
    return b if a is None else a if b is None else a & b


def copies_needed(rows, cols):
    return 128 + 4 * (rows + cols)


def refine_kernel(field_hbm, probe_hbm, coeffs_hbm, pats_hbm, offs, left_hbm, right_hbm,
                  field_out, coeffs_out,
                  ext, grads, gext, pads, psi, phi, highs, lows, probe, coeffs, pats, pats_nat, left, right,
                  stats, half_sums, col_sums, shard, z_sums, new_coeffs,
                  folds, got_x, got_g, relay_in, relay_g, last_x, last_g, relay_last, base, gtile,
                  sq_mine, sq_cols, sq_part, sq_rows, woven,
                  local_sem, send_sem, recv_sem):
    rows, cols = lax.axis_size("row"), lax.axis_size("col")
    r, c = lax.axis_index("row"), lax.axis_index("col")
    depth = rows // 2
    k, z = lax.rem(r, 2), lax.div(r, 2)
    count = pats.shape[0]
    width = probe.shape[1]
    half = width // 2
    size = ext.shape[2]
    tile = size - width
    top = half + tile
    net = Copies(send_sem, recv_sem)

    partner = r + 1 - 2 * k
    beyond = r - 1 + 2 * k
    has_z = (beyond >= 0) & (beyond < rows)
    beyond = lax.rem(beyond + rows, rows)
    odd_c = lax.rem(c, 2)
    step_g = 2 * odd_c - 1
    has_g = (c + step_g >= 0) & (c + step_g < cols)
    has_r = (c - 2 * step_g >= 0) & (c - 2 * step_g < cols)
    col_x = c - step_g
    col_g = lax.rem(c + step_g + cols, cols)
    col_r = lax.rem(c + 2 * step_g + 2 * cols, cols)

    barrier = pltpu.get_barrier_semaphore()
    greeted = 0
    for axis, length, here in (("col", cols, c), ("row", rows, r)):
        for distance in range(1, length):
            other = lax.rem(here + distance, length)
            pl.semaphore_signal(
                barrier, inc=1, device_id=(other, c) if axis == "row" else (r, other),
                device_id_type=pl.DeviceIdType.MESH,
            )
            greeted += 1

    inner = pl.ds(half, tile)
    loads = []

    def load(source, target):
        copy = pltpu.make_async_copy(source, target, local_sem.at[len(loads)])
        copy.start()
        loads.append(copy)
        return copy

    field_loads = [
        load(field_hbm.at[:, :, pl.ds(b * LANES, LANES)], ext.at[:, 1 + b, inner, :]) for b in (0, 1)
    ]
    pats_load = load(pats_hbm.at[0, 0], pats_nat)
    coeffs_load = load(coeffs_hbm, new_coeffs.at[2])
    left_load = load(left_hbm, left)
    right_load = load(right_hbm, right)
    probe_load = load(probe_hbm, probe)

    for edge, b in ((c == 0, 0), (c == cols - 1, 3)):
        @pl.when(edge)
        def _():
            ext[:, b] = jnp.zeros((2, size, LANES), F32)
            gext[:, b] = jnp.zeros((2, size, LANES), F32)
    for edge, start in ((r == 0, 0), (r == rows - 1, top)):
        @pl.when(edge)
        def _():
            ext[:, :, pl.ds(start, half), :] = jnp.zeros((2, 4, half, LANES), F32)
            gext[:, :, pl.ds(start, half), :] = jnp.zeros((2, 4, half, LANES), F32)

    def clear(p, carry):
        for part in (0, 1):
            for b in (0, 4):
                pads[p, part, b] = jnp.zeros((3 * width, LANES), F32)
            for b in (1, 2, 3):
                for start in (0, 2 * width):
                    pads[p, part, b, pl.ds(start, width), :] = jnp.zeros((width, LANES), F32)
        return carry

    lax.fori_loop(0, count, clear, 0)
    for copy in field_loads:
        copy.wait()
    pl.semaphore_wait(barrier, greeted)

    def rows_of(which):
        return half * (1 - k) if which == 0 else half * k

    def side_row(which):
        return top * k if which == 0 else top * (1 - k)

    def edge_row(which):
        return top * (1 - k) if which == 0 else top * k

    def at(start, length):
        return pl.ds(pl.multiple_of(start, 8), length)

    side_dev = (partner, beyond)
    side_has = (None, has_z)

    ends = []
    for which in (1, 0):
        mine = at(half + rows_of(which), half)
        there = at(side_row(which), half)
        ends.append(net.make(ext.at[:, pl.ds(1, 2), mine, :], ext.at[:, pl.ds(1, 2), there, :],
                             row=side_dev[which], sends=side_has[which], gets=side_has[which]).start())

    edge_x, edge_g = 2 - odd_c, 1 + odd_c
    out_x, out_g = 3 * (1 - odd_c), 3 * odd_c
    far_x, far_g = 3 * odd_c, 3 * (1 - odd_c)
    quarter = half // 2
    first_units = [(1, 0), (1, 1), (0, 0), (0, 1)]

    def exchange(units, sources, targets, relays):
        made = {}
        for n, unit in enumerate(units):
            sx, sg1, sg2 = sources(*unit)
            tx, tg1, tg2 = targets(*unit)
            made[unit] = (
                net.make(sx, tx, col=col_x),
                net.make(sg1, tg1, col=col_g, sends=has_g, gets=has_g),
                net.make(sg2, relays.at[n], col=col_r, sends=has_g, gets=has_r),
                net.make(relays.at[n], tg2, col=col_x, sends=has_r, gets=has_g),
            )
        return made

    def push(copies):
        copies[2].start()
        copies[0].start()
        copies[1].start()

    def hand_on(copies):
        copies[2].arrived()
        copies[3].start()

    def first_sources(which, part):
        start = half + rows_of(which)
        return (ext.at[part, edge_x, at(start, half), :],
                ext.at[part, edge_g, at(start, quarter), :],
                ext.at[part, edge_g, at(start + quarter, quarter), :])

    def first_targets(which, part):
        start = half + rows_of(which)
        return (ext.at[part, far_x, at(start, half), :],
                ext.at[part, far_g, at(start, quarter), :],
                ext.at[part, far_g, at(start + quarter, quarter), :])

    side = exchange(first_units, first_sources, first_targets, relay_in)
    for unit in first_units:
        push(side[unit])

    def reorder(full):
        part = dot(jnp.concatenate(split3(full), axis=1), right[4])
        return dot(left[4], jnp.concatenate(split3(part), axis=0))

    pats_load.wait()
    left_load.wait()
    right_load.wait()

    def reorder_pats(p, carry):
        pats[p] = reorder(pats_nat[p])
        return carry

    lax.fori_loop(0, count, reorder_pats, 0)
    hand_on(side[first_units[0]])
    coeffs_load.wait()
    for i in range(3):
        coeffs[i] = reorder(new_coeffs[2, i])
    for unit in first_units[1:]:
        hand_on(side[unit])
    probe_load.wait()

    corners = []
    for which, part in first_units:
        mine = at(half + rows_of(which), half)
        there = at(side_row(which), half)
        for arrivals, b, has in (((0,), out_x, None), ((1, 3), out_g, has_g)):
            for i in arrivals:
                side[(which, part)][i].arrived()
            cond = both(has, side_has[which])
            corners.append(net.make(ext.at[part, b, mine, :], ext.at[part, b, there, :],
                                    row=side_dev[which], sends=cond, gets=cond).start())
    for copy in ends + corners:
        copy.arrived()

    lane = lax.broadcasted_iota(jnp.int32, (1, LANES), 1)

    def place(p):
        oy, ox = offs[0, 0, p, 0], offs[0, 0, p, 1]
        block = lax.div(ox, LANES)
        return oy, block, ox - block * LANES

    def forward(source, into):
        def visit(p, carry):
            oy, block, shift = place(p)
            window = []
            keep = lane < LANES - shift
            for part in (0, 1):
                turned = [
                    pltpu.roll(source[part, block + j, pl.ds(oy, width), :], lax.rem(LANES - shift, LANES), axis=1)
                    for j in range(3)
                ]
                window.append([jnp.where(keep, turned[j], turned[j + 1]) for j in (0, 1)])
            sums, difs = [[], []], [[], []]
            for h in (0, 1):
                pr, pi = probe[0, :, h * LANES:(h + 1) * LANES], probe[1, :, h * LANES:(h + 1) * LANES]
                wr, wi = window[0][h], window[1][h]
                for part, x in ((0, pr * wr - pi * wi), (1, pr * wi + pi * wr)):
                    sums[part].append(x[:half] + x[half:])
                    difs[part].append(x[:half] - x[half:])
            bands = []
            for parity, group in ((0, sums), (1, difs)):
                stack = jnp.concatenate([jnp.concatenate(group[part], axis=1) for part in (0, 1)], axis=0)
                bands.append(from_left(left[parity], stack))
            re = jnp.concatenate([bands[0][:half], bands[1][:half]], axis=0)
            im = jnp.concatenate([bands[0][half:], bands[1][half:]], axis=0)
            plus = jnp.concatenate([re[:, :half] + re[:, half:], im[:, :half] + im[:, half:]], axis=1)
            minus = jnp.concatenate([re[:, :half] - re[:, half:], im[:, :half] - im[:, half:]], axis=1)
            into[p, 0] = from_right(plus, right[0])
            into[p, 1] = from_right(minus, right[1])
            return carry

        lax.fori_loop(0, count, visit, 0, unroll=True)

    def detect(turn, response, start, rate):
        def chunk(i, carry):
            here = pl.ds(pl.multiple_of(start + i * CHUNK, CHUNK), CHUNK)
            for parity in (0, 1):
                span = slice(parity * LANES, (parity + 1) * LANES)
                lin, quad, cubic = (response[j, here, span] for j in range(3))
                sums = [jnp.zeros((CHUNK, LANES), F32)] * 6
                for p in range(count):
                    wr, wi = psi[p, parity, here, :LANES], psi[p, parity, here, LANES:]
                    if rate is not None:
                        wr -= rate * phi[p, parity, here, :LANES]
                        wi -= rate * phi[p, parity, here, LANES:]
                    inten = wr * wr + wi * wi
                    error = inten * (lin + inten * (quad + inten * cubic)) - pats[p, here, span]
                    weight = 2.0 * error * (lin + inten * (2.0 * quad + 3.0 * cubic * inten))
                    squared = inten * inten
                    cubed = squared * inten
                    terms = (error * inten, error * squared, error * cubed,
                             squared, squared * squared, cubed * cubed)
                    sums = [a + b for a, b in zip(sums, terms)]
                    for j, part in ((0, weight * wr), (1, weight * wi)):
                        high, low = split(part)
                        highs[p, parity, here, j * LANES:(j + 1) * LANES] = high
                        lows[p, parity, here, j * LANES:(j + 1) * LANES] = low
                for j in range(6):
                    stats[turn, j, here, span] = sums[j]
            return carry

        lax.fori_loop(0, half // CHUNK, chunk, 0)

    def backward():
        def visit(p, carry):
            _, _, shift = place(p)
            bands = []
            for parity in (0, 1):
                high, low = highs[p, parity], lows[p, parity]
                bands.append(dot(jnp.concatenate([high, low, high], axis=1), right[2 + parity]))
            plus, minus = bands[0] + bands[1], bands[0] - bands[1]
            re = jnp.concatenate([plus[:, :half], minus[:, :half]], axis=1)
            im = jnp.concatenate([plus[:, half:], minus[:, half:]], axis=1)
            bands = []
            for parity in (0, 1):
                rows_in = slice(parity * half, (parity + 1) * half)
                bands.append(from_left(left[2 + parity], jnp.concatenate([re[rows_in], im[rows_in]], axis=0)))
            plus, minus = bands[0] + bands[1], bands[0] - bands[1]
            xr = jnp.concatenate([plus[:half], minus[:half]], axis=0)
            xi = jnp.concatenate([plus[half:], minus[half:]], axis=0)
            pr, pi = probe[0], probe[1]
            keep = lane >= shift
            for part, g in ((0, pr * xr + pi * xi), (1, pr * xi - pi * xr)):
                a = pltpu.roll(g[:, :LANES], shift, axis=1)
                b = pltpu.roll(g[:, LANES:], shift, axis=1)
                zero = jnp.zeros_like(a)
                pads[p, part, 1, pl.ds(width, width), :] = jnp.where(keep, a, zero)
                pads[p, part, 2, pl.ds(width, width), :] = jnp.where(keep, b, a)
                pads[p, part, 3, pl.ds(width, width), :] = jnp.where(keep, zero, b)
            return carry

        lax.fori_loop(0, count, visit, 0, unroll=True)

    def gather(turn, start, length):
        for part in (0, 1):
            for b in range(4):
                total = 0.0
                for p in range(count):
                    oy, block, _ = place(p)
                    total += pads[p, part, b + 1 - block, pl.ds(width - oy + start, length), :]
                grads[turn, part, b, pl.ds(start, length), :] = total

    rows1 = width // 2
    rows2, rows3 = shard.shape[2], z_sums.shape[3]
    cut = rows3 < rows2

    class Sums:
        def __init__(self, turn, old, final):
            self.turn, self.old, self.final = turn, old, final

        def pair(self):
            t = self.turn
            self.first = net.make(stats.at[t, :, at((1 - k) * rows1, rows1), :], half_sums.at[t], row=partner).start()

        def over_cols(self):
            t = self.turn
            self.first.arrived()
            half_sums[t] += stats[t, :, at(k * rows1, rows1), :]
            self.col_copies = []
            for d in range(1, cols):
                other = lax.rem(c + d, cols)
                self.col_copies.append(net.make(half_sums.at[t, :, at(other * rows2, rows2), :],
                                                col_sums.at[t, d - 1], col=other).start())

        def over_z(self):
            t = self.turn
            for copy in self.col_copies:
                copy.arrived()
            shard[t] = half_sums[t, :, at(c * rows2, rows2), :] + sum(col_sums[t, d] for d in range(cols - 1))
            self.z_copies = []
            for d in range(1, depth):
                other = lax.rem(z + d, depth)
                source = shard.at[t, :, at(other * rows3, rows3), :] if cut else shard.at[t]
                self.z_copies.append(net.make(source, z_sums.at[t, d - 1], row=2 * other + k).start())

        def update(self):
            t = self.turn
            for copy in self.z_copies:
                copy.arrived()
            own = shard[t, :, at(z * rows3, rows3), :] if cut else shard[t]
            sums = own + sum(z_sums[t, i] for i in range(depth - 1))
            self.base2 = k * rows1 + c * rows2
            self.base3 = self.base2 + z * rows3 if cut else self.base2
            fresh = self.old[:, at(self.base3, rows3), :] - sums[:3] / (sums[3:] + RIDGE)
            if self.final:
                flat = fresh.reshape(3 * rows3, width)
                fresh = dot(jnp.concatenate(split3(flat), axis=1), right[5]).reshape(3, rows3, width)
            new_coeffs[t, :, at(self.base3, rows3), :] = fresh
            self.back = []
            if cut:
                ready = new_coeffs.at[t, :, at(self.base3, rows3), :]
                for d in range(1, depth):
                    self.back.append(net.make(ready, ready, row=2 * lax.rem(z + d, depth) + k).start())

        def spread(self):
            t = self.turn
            for copy in self.back:
                copy.arrived()
            ready = new_coeffs.at[t, :, at(self.base2, rows2), :]
            self.wide = [net.make(ready, ready, col=lax.rem(c + d, cols)).start() for d in range(1, cols)]

        def swap(self):
            for copy in self.wide:
                copy.arrived()
            ready = new_coeffs.at[self.turn, :, at(k * rows1, rows1), :]
            self.end = net.make(ready, ready, row=partner).start()

        def done(self):
            self.end.arrived()

    class Norm:
        def __init__(self, turn):
            self.turn = turn

        def over_cols(self, square):
            t = self.turn
            sq_mine[t] = square
            self.col_copies = [
                net.make(sq_mine.at[t], sq_cols.at[t, d - 1], col=lax.rem(c + d, cols)).start() for d in range(1, cols)
            ]

        def over_rows(self):
            t = self.turn
            for copy in self.col_copies:
                copy.arrived()
            sq_part[t] = sq_mine[t] + sum(sq_cols[t, d] for d in range(cols - 1))
            self.row_copies = [
                net.make(sq_part.at[t], sq_rows.at[t, d - 1], row=lax.rem(r + d, rows)).start() for d in range(1, rows)
            ]

        def rate(self):
            t = self.turn
            for copy in self.row_copies:
                copy.arrived()
            square = sq_part[t] + sum(sq_rows[t, d] for d in range(rows - 1))
            total = 2.0 * tile * tile * rows * cols
            return STEP_RATE / jnp.sqrt(jnp.sum(square, keepdims=True) / total + EPSILON)

    def fold_rows(turn):
        made = {}
        for which in (1, 0):
            for part in (0, 1):
                made[(which, part)] = net.make(
                    grads.at[turn, part, :, at(edge_row(which), half), :], folds.at[turn, which, part],
                    row=side_dev[which], sends=side_has[which], gets=side_has[which],
                ).start()
        return made

    def add_fold(turn, made, which, part):
        made[(which, part)].arrived()

        def add():
            grads[turn, part, :, at(half + rows_of(which), half), :] += folds[turn, which, part]

        when(side_has[which], add)

    block_x, block_g = 2 * (1 - odd_c), 2 * odd_c

    forward(ext, psi)
    sums0 = Sums(0, coeffs, False)
    detect(0, coeffs, half * (1 - k), None)
    sums0.pair()
    detect(0, coeffs, half * k, None)
    sums0.over_cols()
    backward()
    gather(0, 0, half)
    gather(0, top, half)
    made = fold_rows(0)
    gather(0, half, tile)

    units = [(0, 0), (1, 0), (1, 1), (0, 1)]

    def mid_sources(which, part):
        here = at(half + rows_of(which), half)
        return (grads.at[0, part, pl.ds(block_x, 2), here, :],
                grads.at[0, part, block_g, here, :],
                grads.at[0, part, block_g + 1, here, :])

    def mid_targets(which, part):
        return got_x.at[which, part], got_g.at[which, part, 0], got_g.at[which, part, 1]

    mids = exchange(units, mid_sources, mid_targets, relay_g)
    sides = []

    def take(unit):
        which, part = unit
        here = at(half + rows_of(which), half)
        mids[unit][0].arrived()
        gext[part, pl.ds(block_x, 2), here, :] = grads[0, part, pl.ds(block_x, 2), here, :] + got_x[which, part]
        mids[unit][1].arrived()
        mids[unit][3].arrived()

        @pl.when(has_g)
        def _():
            gext[part, pl.ds(block_g, 2), here, :] = grads[0, part, pl.ds(block_g, 2), here, :] + got_g[which, part]

        @pl.when(jnp.logical_not(has_g))
        def _():
            gext[part, edge_g, here, :] = grads[0, part, edge_g, here, :]

        sides.append(net.make(
            gext.at[part, :, here, :], gext.at[part, :, at(side_row(which), half), :],
            row=side_dev[which], sends=side_has[which], gets=side_has[which],
        ).start())

    add_fold(0, made, *units[0])
    push(mids[units[0]])
    add_fold(0, made, *units[1])
    push(mids[units[1]])
    hand_on(mids[units[0]])
    add_fold(0, made, *units[2])
    push(mids[units[2]])
    hand_on(mids[units[1]])
    add_fold(0, made, *units[3])
    push(mids[units[3]])
    sums0.over_z()
    hand_on(mids[units[2]])
    take(units[0])
    sums0.update()
    hand_on(mids[units[3]])
    take(units[1])
    sums0.spread()
    take(units[2])
    take(units[3])
    sums0.swap()

    def squares(blocks):
        total = 0.0
        for block in blocks:
            total += jnp.sum((block * block).reshape(-1, 8, LANES), axis=0)
        return total

    norm0 = Norm(0)
    norm0.over_cols(squares([gext[part, b, inner, :] for part in (0, 1) for b in (1, 2)]))
    for copy in sides:
        copy.arrived()
    norm0.over_rows()

    forward(gext, phi)
    rate0 = norm0.rate()
    sums0.done()
    sums1 = Sums(1, new_coeffs.at[0], True)
    detect(1, new_coeffs.at[0], half * (1 - k), rate0)
    sums1.pair()
    detect(1, new_coeffs.at[0], half * k, rate0)
    sums1.over_cols()
    backward()
    gather(1, 0, half)
    gather(1, top, half)
    made = fold_rows(1)
    gather(1, half, tile)

    units = [(0, 0), (0, 1), (1, 0), (1, 1)]

    def last_sources(which, part):
        start = half + rows_of(which)
        return (grads.at[1, part, out_x, at(start, half), :],
                grads.at[1, part, out_g, at(start, quarter), :],
                grads.at[1, part, out_g, at(start + quarter, quarter), :])

    def last_targets(which, part):
        return (last_x.at[which, part], last_g.at[which, part, pl.ds(0, quarter), :],
                last_g.at[which, part, pl.ds(quarter, quarter), :])

    lasts = exchange(units, last_sources, last_targets, relay_last)
    for part in (0, 1):
        for b in (0, 1):
            base[part, b] = ext[part, 1 + b, inner, :] - rate0 * gext[part, 1 + b, inner, :]
    for n, unit in enumerate(units):
        add_fold(1, made, *unit)
        push(lasts[unit])
        if n:
            hand_on(lasts[units[n - 1]])
    hand_on(lasts[units[3]])
    sums1.over_z()
    square = 0.0
    for which, part in units:
        here = at(half + rows_of(which), half)
        there = at(rows_of(which), half)
        lasts[(which, part)][0].arrived()
        lasts[(which, part)][1].arrived()
        lasts[(which, part)][3].arrived()
        mine = grads[1, part, edge_x, here, :] + last_x[which, part]
        gtile[part, edge_x - 1, there, :] = mine
        square += squares([mine])

        @pl.when(has_g)
        def _():
            gtile[part, edge_g - 1, there, :] = grads[1, part, edge_g, here, :] + last_g[which, part]

        @pl.when(jnp.logical_not(has_g))
        def _():
            gtile[part, edge_g - 1, there, :] = grads[1, part, edge_g, here, :]

        square += squares([gtile[part, edge_g - 1, there, :]])
    norm1 = Norm(1)
    norm1.over_cols(square)
    sums1.update()
    norm1.over_rows()
    sums1.spread()
    rate1 = norm1.rate()
    for part in (0, 1):
        for b in (0, 1):
            field_out[part, :, b * LANES:(b + 1) * LANES] = base[part, b] - rate1 * gtile[part, b]
    sums1.swap()
    sums1.done()
    for i in range(3):
        for b in (0, 1):
            span = slice(b * LANES, (b + 1) * LANES)
            for parity in (0, 1):
                woven[i, b, pl.ds(parity, half, stride=2), :] = new_coeffs[1, i, parity * half:(parity + 1) * half, span]
            coeffs_out[i, :, span] = woven[i, b]
    net.finish()


def local(object_field, probe, coeffs, patterns, offsets):
    rows, cols = lax.axis_size("row"), lax.axis_size("col")
    depth = rows // 2
    count, width = patterns.shape[2], probe.shape[1]
    half = width // 2
    tile = object_field.shape[1]
    size = tile + width
    rows1 = width // 2
    rows2 = rows1 // cols
    rows3 = rows2 // depth if rows2 % (8 * depth) == 0 else rows2
    left, right = dft_halves(width)
    vmem = pl.BlockSpec(memory_space=pltpu.VMEM)
    hbm = pl.BlockSpec(memory_space=pl.ANY)
    semaphores = copies_needed(rows, cols)
    extended = (2, size // LANES, size, LANES)
    freq = (count, 2, width, width)
    return pl.pallas_call(
        refine_kernel,
        out_shape=(
            jax.ShapeDtypeStruct((2, tile, tile), F32),
            jax.ShapeDtypeStruct(coeffs.shape, F32),
        ),
        in_specs=[hbm] * 4 + [pl.BlockSpec(memory_space=pltpu.SMEM)] + [hbm] * 2,
        out_specs=(vmem, vmem),
        scratch_shapes=[
            pltpu.VMEM(extended, F32),
            pltpu.VMEM((2,) + extended, F32),
            pltpu.VMEM(extended, F32),
            pltpu.VMEM((count, 2, 5, 3 * width, LANES), F32),
            pltpu.VMEM(freq, F32),
            pltpu.VMEM(freq, F32),
            pltpu.VMEM(freq, BF16),
            pltpu.VMEM(freq, BF16),
            pltpu.VMEM((2, width, width), F32),
            pltpu.VMEM((3, width, width), F32),
            pltpu.VMEM((count, width, width), F32),
            pltpu.VMEM((count, width, width), F32),
            pltpu.VMEM(left.shape, BF16),
            pltpu.VMEM(right.shape, BF16),
            pltpu.VMEM((2, 6, width, width), F32),
            pltpu.VMEM((2, 6, rows1, width), F32),
            pltpu.VMEM((2, cols - 1, 6, rows2, width), F32),
            pltpu.VMEM((2, 6, rows2, width), F32),
            pltpu.VMEM((2, depth - 1, 6, rows3, width), F32),
            pltpu.VMEM((3, 3, width, width), F32),
            pltpu.VMEM((2, 2, 2, size // LANES, half, LANES), F32),
            pltpu.VMEM((2, 2, 2, half, LANES), F32),
            pltpu.VMEM((2, 2, 2, half, LANES), F32),
            pltpu.VMEM((4, half // 2, LANES), F32),
            pltpu.VMEM((4, half, LANES), F32),
            pltpu.VMEM((2, 2, half, LANES), F32),
            pltpu.VMEM((2, 2, half, LANES), F32),
            pltpu.VMEM((4, half // 2, LANES), F32),
            pltpu.VMEM((2, 2, tile, LANES), F32),
            pltpu.VMEM((2, 2, tile, LANES), F32),
            pltpu.VMEM((2, 8, LANES), F32),
            pltpu.VMEM((2, cols - 1, 8, LANES), F32),
            pltpu.VMEM((2, 8, LANES), F32),
            pltpu.VMEM((2, rows - 1, 8, LANES), F32),
            pltpu.VMEM((3, width // LANES, width, LANES), F32),
            pltpu.SemaphoreType.DMA((8,)),
            pltpu.SemaphoreType.DMA((semaphores,)),
            pltpu.SemaphoreType.DMA((semaphores,)),
        ],
        compiler_params=pltpu.CompilerParams(
            collective_id=0, has_side_effects=True, vmem_limit_bytes=58 * 1024 * 1024
        ),
        name="refine",
    )(object_field, probe, coeffs, patterns, offsets, left, right)


def solution(mesh):
    placed = (
        P(None, "row", "col"),
        P(),
        P(),
        P("row", "col", None, None, None),
        P("row", "col", None, None),
    )
    return jax.shard_map(
        local, mesh=mesh, in_specs=placed, out_specs=(P(None, "row", "col"), P()), check_vma=False
    )
```

time: 151 us -> 106 us (0.70)
  Pallas kernels: 140 us -> 100 us
  local copies, waits for them, and re-layouts: 9.16 us -> 5.27 us
    pallas_call x5 -> x1, Pallas kernels: 140 us -> 100 us  [local(): pl.pallas_call(refine_kernel, out_shape=(jax.ShapeDtypeStruct((2, tile, t...]
    unnamed x32 -> x3, local copies, waits for them, and re-layouts: 8.24 us -> 5.27 us
where the time goes in v1:
time: 106 us
  Pallas kernels  100 us (94%)
  local copies, waits for them, and re-layouts  5.27 us (5%)
    pallas_call x1, Pallas kernels, local(): pl.pallas_call(refine_kernel, out_shape=(jax.ShapeDtypeStruct((2, tile, t...  100 us
    unnamed x3, local copies, waits for them, and re-layouts  5.27 us

profile of v1, /device:TPU:0, one launch (start us, length us, event | category | flops | bytes accessed | tf_op | source)
XLA Modules:
  0.0 105.9 jit_solution(10143575235781089181)
XLA Ops:
  0.6 1.3 %copy.9.offs = s32[1,1,4,2]{3,2,1,0:T(4,128)} copy(s32[1,1,4,2]{2,3,1,0:T(2,128)} %param.11) | data formatting | bytes 64 | tf_op args[4]
  2.0 100.0 %refine.1 = (f32[2,256,256]{2,1,0:T(8,128)}, f32[3,256,256]{2,1,0:T(8,128)}) custom-call(f32[2,256,256]{2,1,0:T(8,128)} %field_hbm.1, f32[2,256,256]{2,1,0:T(8,128)} %probe_hbm.1, f32[3,256,256]{2,1,0:T(8,128)} %coeffs_hbm.1, f32[1,1,4,256,256]{4,3,2,1,0:T(8,128)} %pats_hbm.1, s32[1,1,4,2]{3,2,1,0:T(4,128)} %copy.9.offs, ...), custom_call_target="tpu_custom_call" | custom-call | tf_op jit(solution)/shard_map/refine/pallas_call | solution.py:705
  101.9 1.9 %copy.12 = f32[2,256,256]{2,1,0:T(8,128)} copy(f32[2,256,256]{2,1,0:T(8,128)} %get-tuple-element.4) | data formatting | bytes 1048576
  103.8 2.1 %copy.13 = f32[3,256,256]{2,1,0:T(8,128)} copy(f32[3,256,256]{2,1,0:T(8,128)} %get-tuple-element.5) | data formatting | bytes 1572864

commit v2 on v1

--- a/solution.py
+++ b/solution.py
@@ -71,7 +71,7 @@
 
 class Copies:
     def __init__(self, send, recv):
-        self.send, self.recv, self.used, self.made = send, recv, 0, []
+        self.send, self.recv, self.used, self.made, self.ended = send, recv, 0, [], 0
 
     def make(self, source, target, row=None, col=None, sends=None, gets=None):
         slot = self.used
@@ -85,9 +85,11 @@
         self.made.append(made)
         return made
 
-    def finish(self):
-        for made in self.made:
+    def finish(self, mark=None):
+        mark = len(self.made) if mark is None else mark
+        for made in self.made[self.ended:mark]:
             made.sent()
+        self.ended = mark
 
 
 def when(condition, act):
@@ -117,15 +119,15 @@
 
 
 def copies_needed(rows, cols):
-    return 128 + 4 * (rows + cols)
+    return 160 + 4 * (rows + cols) + rows * cols
 
 
 def refine_kernel(field_hbm, probe_hbm, coeffs_hbm, pats_hbm, offs, left_hbm, right_hbm,
                   field_out, coeffs_out,
-                  ext, grads, gext, pads, psi, phi, highs, lows, probe, coeffs, pats, pats_nat, left, right,
+                  ext, grads, gext, pads, psi, phi, highs, lows, probe, coeffs, pats, left, right,
                   stats, half_sums, col_sums, shard, z_sums, new_coeffs,
                   folds, got_x, got_g, relay_in, relay_g, last_x, last_g, relay_last, base, gtile,
-                  sq_mine, sq_cols, sq_part, sq_rows, woven,
+                  sq_mine, sq_pair, sq_part, sq_all, woven, acc,
                   local_sem, send_sem, recv_sem):
     rows, cols = lax.axis_size("row"), lax.axis_size("col")
     r, c = lax.axis_index("row"), lax.axis_index("col")
@@ -151,16 +153,21 @@
     col_g = lax.rem(c + step_g + cols, cols)
     col_r = lax.rem(c + 2 * step_g + 2 * cols, cols)
 
+    def chip(dz, dc):
+        return 2 * lax.rem(z + dz, depth) + k, lax.rem(c + dc, cols)
+
+    others = [(dz, dc) for dz in range(depth) for dc in range(cols) if dz or dc]
+
     barrier = pltpu.get_barrier_semaphore()
-    greeted = 0
-    for axis, length, here in (("col", cols, c), ("row", rows, r)):
-        for distance in range(1, length):
-            other = lax.rem(here + distance, length)
-            pl.semaphore_signal(
-                barrier, inc=1, device_id=(other, c) if axis == "row" else (r, other),
-                device_id_type=pl.DeviceIdType.MESH,
-            )
-            greeted += 1
+
+    def greet(row, col):
+        pl.semaphore_signal(barrier, inc=1, device_id=(row, col), device_id_type=pl.DeviceIdType.MESH)
+
+    for dz, dc in others:
+        greet(*chip(dz, dc))
+    greet(partner, c)
+    when(has_z, lambda: greet(beyond, c))
+    greeted = len(others) + 1 + has_z.astype(jnp.int32)
 
     inner = pl.ds(half, tile)
     loads = []
@@ -174,8 +181,8 @@
     field_loads = [
         load(field_hbm.at[:, :, pl.ds(b * LANES, LANES)], ext.at[:, 1 + b, inner, :]) for b in (0, 1)
     ]
-    pats_load = load(pats_hbm.at[0, 0], pats_nat)
-    coeffs_load = load(coeffs_hbm, new_coeffs.at[2])
+    pats_load = load(pats_hbm.at[0, 0], pats)
+    coeffs_load = load(coeffs_hbm, acc)
     left_load = load(left_hbm, left)
     right_load = load(right_hbm, right)
     probe_load = load(probe_hbm, probe)
@@ -268,47 +275,61 @@
                 ext.at[part, far_g, at(start + quarter, quarter), :])
 
     side = exchange(first_units, first_sources, first_targets, relay_in)
+    def straight(unit):
+        side[unit][0].start()
+        side[unit][1].start()
+
     for unit in first_units:
-        push(side[unit])
+        side[unit][2].start()
+    for unit in first_units[:3]:
+        straight(unit)
 
     def reorder(full):
         part = dot(jnp.concatenate(split3(full), axis=1), right[4])
         return dot(left[4], jnp.concatenate(split3(part), axis=0))
 
-    pats_load.wait()
-    left_load.wait()
-    right_load.wait()
-
     def reorder_pats(p, carry):
-        pats[p] = reorder(pats_nat[p])
+        pats[p] = reorder(pats[p])
         return carry
 
-    lax.fori_loop(0, count, reorder_pats, 0)
+    for copy in (pats_load, left_load, right_load, coeffs_load, probe_load):
+        copy.wait()
+    lax.fori_loop(0, count // 2, reorder_pats, 0)
     hand_on(side[first_units[0]])
-    coeffs_load.wait()
+    hand_on(side[first_units[1]])
+    straight(first_units[3])
+    lax.fori_loop(count // 2, count, reorder_pats, 0)
+    hand_on(side[first_units[2]])
+    hand_on(side[first_units[3]])
     for i in range(3):
-        coeffs[i] = reorder(new_coeffs[2, i])
-    for unit in first_units[1:]:
-        hand_on(side[unit])
-    probe_load.wait()
+        full = reorder(acc[i])
+        for parity in (0, 1):
+            coeffs[parity, i] = full[:, parity * LANES:(parity + 1) * LANES]
 
     corners = []
-    for which, part in first_units:
+
+    def corner(unit, arrivals, b, has):
+        which, part = unit
+        for i in arrivals:
+            side[unit][i].arrived()
+        cond = both(has, side_has[which])
         mine = at(half + rows_of(which), half)
         there = at(side_row(which), half)
-        for arrivals, b, has in (((0,), out_x, None), ((1, 3), out_g, has_g)):
-            for i in arrivals:
-                side[(which, part)][i].arrived()
-            cond = both(has, side_has[which])
-            corners.append(net.make(ext.at[part, b, mine, :], ext.at[part, b, there, :],
-                                    row=side_dev[which], sends=cond, gets=cond).start())
+        corners.append(net.make(ext.at[part, b, mine, :], ext.at[part, b, there, :],
+                                row=side_dev[which], sends=cond, gets=cond).start())
+
+    for pair in (first_units[:2], first_units[2:]):
+        for unit in pair:
+            corner(unit, (0,), out_x, None)
+        for unit in pair:
+            corner(unit, (1, 3), out_g, has_g)
     for copy in ends + corners:
         copy.arrived()
 
     lane = lax.broadcasted_iota(jnp.int32, (1, LANES), 1)
 
     def place(p):
-        oy, ox = offs[0, 0, p, 0], offs[0, 0, p, 1]
+        oy, ox = offs[0, 0, 0, p], offs[0, 0, 1, p]
         block = lax.div(ox, LANES)
         return oy, block, ox - block * LANES
 
@@ -344,35 +365,35 @@
 
         lax.fori_loop(0, count, visit, 0, unroll=True)
 
-    def detect(turn, response, start, rate):
+    def detect(turn, parity, response, rate):
+        span = slice(parity * LANES, (parity + 1) * LANES)
+
         def chunk(i, carry):
-            here = pl.ds(pl.multiple_of(start + i * CHUNK, CHUNK), CHUNK)
-            for parity in (0, 1):
-                span = slice(parity * LANES, (parity + 1) * LANES)
-                lin, quad, cubic = (response[j, here, span] for j in range(3))
-                sums = [jnp.zeros((CHUNK, LANES), F32)] * 6
-                for p in range(count):
-                    wr, wi = psi[p, parity, here, :LANES], psi[p, parity, here, LANES:]
-                    if rate is not None:
-                        wr -= rate * phi[p, parity, here, :LANES]
-                        wi -= rate * phi[p, parity, here, LANES:]
-                    inten = wr * wr + wi * wi
-                    error = inten * (lin + inten * (quad + inten * cubic)) - pats[p, here, span]
-                    weight = 2.0 * error * (lin + inten * (2.0 * quad + 3.0 * cubic * inten))
-                    squared = inten * inten
-                    cubed = squared * inten
-                    terms = (error * inten, error * squared, error * cubed,
-                             squared, squared * squared, cubed * cubed)
-                    sums = [a + b for a, b in zip(sums, terms)]
-                    for j, part in ((0, weight * wr), (1, weight * wi)):
-                        high, low = split(part)
-                        highs[p, parity, here, j * LANES:(j + 1) * LANES] = high
-                        lows[p, parity, here, j * LANES:(j + 1) * LANES] = low
-                for j in range(6):
-                    stats[turn, j, here, span] = sums[j]
+            here = pl.ds(pl.multiple_of(i * CHUNK, CHUNK), CHUNK)
+            lin, quad, cubic = (response[parity, j, here, :] for j in range(3))
+            sums = [jnp.zeros((CHUNK, LANES), F32)] * 6
+            for p in range(count):
+                wr, wi = psi[p, parity, here, :LANES], psi[p, parity, here, LANES:]
+                if rate is not None:
+                    wr -= rate * phi[p, parity, here, :LANES]
+                    wi -= rate * phi[p, parity, here, LANES:]
+                inten = wr * wr + wi * wi
+                error = inten * (lin + inten * (quad + inten * cubic)) - pats[p, here, span]
+                weight = 2.0 * error * (lin + inten * (2.0 * quad + 3.0 * cubic * inten))
+                squared = inten * inten
+                cubed = squared * inten
+                terms = (error * inten, error * squared, error * cubed,
+                         squared, squared * squared, cubed * cubed)
+                sums = [a + b for a, b in zip(sums, terms)]
+                for j, part in ((0, weight * wr), (1, weight * wi)):
+                    high, low = split(part)
+                    highs[p, parity, here, j * LANES:(j + 1) * LANES] = high
+                    lows[p, parity, here, j * LANES:(j + 1) * LANES] = low
+            for j in range(6):
+                stats[turn, parity, j, here, :] = sums[j]
             return carry
 
-        lax.fori_loop(0, half // CHUNK, chunk, 0)
+        lax.fori_loop(0, width // CHUNK, chunk, 0, unroll=2)
 
     def backward():
         def visit(p, carry):
@@ -414,68 +435,64 @@
                 grads[turn, part, b, pl.ds(start, length), :] = total
 
     rows1 = width // 2
-    rows2, rows3 = shard.shape[2], z_sums.shape[3]
+    rows2, rows3 = shard.shape[3], z_sums.shape[4]
     cut = rows3 < rows2
 
     class Sums:
-        def __init__(self, turn, old, final):
-            self.turn, self.old, self.final = turn, old, final
+        def __init__(self, turn, parity, old):
+            self.at, self.old = (turn, parity), old
+            self.base2 = k * rows1 + c * rows2
+            self.base3 = self.base2 + z * rows3 if cut else self.base2
 
         def pair(self):
-            t = self.turn
-            self.first = net.make(stats.at[t, :, at((1 - k) * rows1, rows1), :], half_sums.at[t], row=partner).start()
+            t = self.at
+            self.first = net.make(stats.at[*t, :, at((1 - k) * rows1, rows1), :], half_sums.at[t], row=partner).start()
 
         def over_cols(self):
-            t = self.turn
+            t = self.at
             self.first.arrived()
-            half_sums[t] += stats[t, :, at(k * rows1, rows1), :]
-            self.col_copies = []
+            half_sums[t] += stats[*t, :, at(k * rows1, rows1), :]
+            self.copies = []
             for d in range(1, cols):
                 other = lax.rem(c + d, cols)
-                self.col_copies.append(net.make(half_sums.at[t, :, at(other * rows2, rows2), :],
-                                                col_sums.at[t, d - 1], col=other).start())
+                self.copies.append(net.make(half_sums.at[*t, :, at(other * rows2, rows2), :],
+                                            col_sums.at[*t, d - 1], col=other).start())
 
         def over_z(self):
-            t = self.turn
-            for copy in self.col_copies:
+            t = self.at
+            for copy in self.copies:
                 copy.arrived()
-            shard[t] = half_sums[t, :, at(c * rows2, rows2), :] + sum(col_sums[t, d] for d in range(cols - 1))
-            self.z_copies = []
+            shard[t] = half_sums[*t, :, at(c * rows2, rows2), :] + sum(col_sums[*t, d] for d in range(cols - 1))
+            self.copies = []
             for d in range(1, depth):
                 other = lax.rem(z + d, depth)
-                source = shard.at[t, :, at(other * rows3, rows3), :] if cut else shard.at[t]
-                self.z_copies.append(net.make(source, z_sums.at[t, d - 1], row=2 * other + k).start())
+                source = shard.at[*t, :, at(other * rows3, rows3), :] if cut else shard.at[t]
+                self.copies.append(net.make(source, z_sums.at[*t, d - 1], row=2 * other + k).start())
 
         def update(self):
-            t = self.turn
-            for copy in self.z_copies:
+            t = self.at
+            for copy in self.copies:
                 copy.arrived()
-            own = shard[t, :, at(z * rows3, rows3), :] if cut else shard[t]
-            sums = own + sum(z_sums[t, i] for i in range(depth - 1))
-            self.base2 = k * rows1 + c * rows2
-            self.base3 = self.base2 + z * rows3 if cut else self.base2
-            fresh = self.old[:, at(self.base3, rows3), :] - sums[:3] / (sums[3:] + RIDGE)
-            if self.final:
-                flat = fresh.reshape(3 * rows3, width)
-                fresh = dot(jnp.concatenate(split3(flat), axis=1), right[5]).reshape(3, rows3, width)
-            new_coeffs[t, :, at(self.base3, rows3), :] = fresh
-            self.back = []
+            own = shard[*t, :, at(z * rows3, rows3), :] if cut else shard[t]
+            sums = own + sum(z_sums[*t, i] for i in range(depth - 1))
+            new_coeffs[*t, :, at(self.base3, rows3), :] = (
+                self.old[t[1], :, at(self.base3, rows3), :] - sums[:3] / (sums[3:] + RIDGE))
+            self.copies = []
             if cut:
-                ready = new_coeffs.at[t, :, at(self.base3, rows3), :]
+                ready = new_coeffs.at[*t, :, at(self.base3, rows3), :]
                 for d in range(1, depth):
-                    self.back.append(net.make(ready, ready, row=2 * lax.rem(z + d, depth) + k).start())
+                    self.copies.append(net.make(ready, ready, row=2 * lax.rem(z + d, depth) + k).start())
 
         def spread(self):
-            t = self.turn
-            for copy in self.back:
+            for copy in self.copies:
                 copy.arrived()
-            ready = new_coeffs.at[t, :, at(self.base2, rows2), :]
-            self.wide = [net.make(ready, ready, col=lax.rem(c + d, cols)).start() for d in range(1, cols)]
+            ready = new_coeffs.at[*self.at, :, at(self.base2, rows2), :]
+            self.copies = [net.make(ready, ready, col=lax.rem(c + d, cols)).start() for d in range(1, cols)]
 
         def swap(self):
-            for copy in self.wide:
+            for copy in self.copies:
                 copy.arrived()
-            ready = new_coeffs.at[self.turn, :, at(k * rows1, rows1), :]
+            ready = new_coeffs.at[*self.at, :, at(k * rows1, rows1), :]
             self.end = net.make(ready, ready, row=partner).start()
 
         def done(self):
@@ -485,27 +502,25 @@
         def __init__(self, turn):
             self.turn = turn
 
-        def over_cols(self, square):
+        def pair(self, square):
             t = self.turn
             sq_mine[t] = square
-            self.col_copies = [
-                net.make(sq_mine.at[t], sq_cols.at[t, d - 1], col=lax.rem(c + d, cols)).start() for d in range(1, cols)
-            ]
-
-        def over_rows(self):
+            self.first = net.make(sq_mine.at[t], sq_pair.at[t], row=partner).start()
+
+        def wide(self):
             t = self.turn
-            for copy in self.col_copies:
-                copy.arrived()
-            sq_part[t] = sq_mine[t] + sum(sq_cols[t, d] for d in range(cols - 1))
-            self.row_copies = [
-                net.make(sq_part.at[t], sq_rows.at[t, d - 1], row=lax.rem(r + d, rows)).start() for d in range(1, rows)
-            ]
+            self.first.arrived()
+            sq_part[t] = sq_mine[t] + sq_pair[t]
+            self.copies = []
+            for i, place in enumerate(others):
+                row, col = chip(*place)
+                self.copies.append(net.make(sq_part.at[t], sq_all.at[t, i], row=row, col=col).start())
 
         def rate(self):
             t = self.turn
-            for copy in self.row_copies:
+            for copy in self.copies:
                 copy.arrived()
-            square = sq_part[t] + sum(sq_rows[t, d] for d in range(rows - 1))
+            square = sq_part[t] + sum(sq_all[t, i] for i in range(len(others)))
             total = 2.0 * tile * tile * rows * cols
             return STEP_RATE / jnp.sqrt(jnp.sum(square, keepdims=True) / total + EPSILON)
 
@@ -530,11 +545,13 @@
     block_x, block_g = 2 * (1 - odd_c), 2 * odd_c
 
     forward(ext, psi)
-    sums0 = Sums(0, coeffs, False)
-    detect(0, coeffs, half * (1 - k), None)
-    sums0.pair()
-    detect(0, coeffs, half * k, None)
-    sums0.over_cols()
+    sums0 = [Sums(0, parity, coeffs) for parity in (0, 1)]
+    detect(0, 0, coeffs, None)
+    sums0[0].pair()
+    detect(0, 1, coeffs, None)
+    sums0[1].pair()
+    sums0[0].over_cols()
+    sums0[1].over_cols()
     backward()
     gather(0, 0, half)
     gather(0, top, half)
@@ -576,26 +593,23 @@
             row=side_dev[which], sends=side_has[which], gets=side_has[which],
         ).start())
 
-    add_fold(0, made, *units[0])
-    push(mids[units[0]])
-    add_fold(0, made, *units[1])
-    push(mids[units[1]])
+    for unit in units:
+        add_fold(0, made, *unit)
+        push(mids[unit])
+    sums0[0].over_z()
     hand_on(mids[units[0]])
-    add_fold(0, made, *units[2])
-    push(mids[units[2]])
     hand_on(mids[units[1]])
-    add_fold(0, made, *units[3])
-    push(mids[units[3]])
-    sums0.over_z()
+    sums0[1].over_z()
     hand_on(mids[units[2]])
+    sums0[0].update()
+    hand_on(mids[units[3]])
     take(units[0])
-    sums0.update()
-    hand_on(mids[units[3]])
+    sums0[1].update()
     take(units[1])
-    sums0.spread()
+    sums0[0].spread()
     take(units[2])
+    sums0[1].spread()
     take(units[3])
-    sums0.swap()
 
     def squares(blocks):
         total = 0.0
@@ -604,19 +618,26 @@
         return total
 
     norm0 = Norm(0)
-    norm0.over_cols(squares([gext[part, b, inner, :] for part in (0, 1) for b in (1, 2)]))
+    mark = len(net.made)
+    norm0.pair(squares([gext[part, b, inner, :] for part in (0, 1) for b in (1, 2)]))
     for copy in sides:
         copy.arrived()
-    norm0.over_rows()
+    norm0.wide()
 
     forward(gext, phi)
+    net.finish(mark)
+    sums0[0].swap()
     rate0 = norm0.rate()
-    sums0.done()
-    sums1 = Sums(1, new_coeffs.at[0], True)
-    detect(1, new_coeffs.at[0], half * (1 - k), rate0)
-    sums1.pair()
-    detect(1, new_coeffs.at[0], half * k, rate0)
-    sums1.over_cols()
+    sums0[0].done()
+    sums1 = [Sums(1, parity, new_coeffs.at[0]) for parity in (0, 1)]
+    detect(1, 0, new_coeffs.at[0], rate0)
+    sums0[1].swap()
+    sums1[0].pair()
+    sums0[1].done()
+    detect(1, 1, new_coeffs.at[0], rate0)
+    sums1[1].pair()
+    sums1[0].over_cols()
+    sums1[1].over_cols()
     backward()
     gather(1, 0, half)
     gather(1, top, half)
@@ -639,15 +660,8 @@
     for part in (0, 1):
         for b in (0, 1):
             base[part, b] = ext[part, 1 + b, inner, :] - rate0 * gext[part, 1 + b, inner, :]
-    for n, unit in enumerate(units):
-        add_fold(1, made, *unit)
-        push(lasts[unit])
-        if n:
-            hand_on(lasts[units[n - 1]])
-    hand_on(lasts[units[3]])
-    sums1.over_z()
-    square = 0.0
-    for which, part in units:
+    def settle(unit):
+        which, part = unit
         here = at(half + rows_of(which), half)
         there = at(rows_of(which), half)
         lasts[(which, part)][0].arrived()
@@ -655,7 +669,7 @@
         lasts[(which, part)][3].arrived()
         mine = grads[1, part, edge_x, here, :] + last_x[which, part]
         gtile[part, edge_x - 1, there, :] = mine
-        square += squares([mine])
+        square = squares([mine])
 
         @pl.when(has_g)
         def _():
@@ -665,23 +679,56 @@
         def _():
             gtile[part, edge_g - 1, there, :] = grads[1, part, edge_g, here, :]
 
-        square += squares([gtile[part, edge_g - 1, there, :]])
+        return square + squares([gtile[part, edge_g - 1, there, :]])
+
+    for unit in units[:2]:
+        add_fold(1, made, *unit)
+        push(lasts[unit])
+    sums1[0].over_z()
+    hand_on(lasts[units[0]])
+    add_fold(1, made, *units[2])
+    push(lasts[units[2]])
+    hand_on(lasts[units[1]])
+    add_fold(1, made, *units[3])
+    push(lasts[units[3]])
+    sums1[1].over_z()
+    hand_on(lasts[units[2]])
+    sums1[0].update()
+    hand_on(lasts[units[3]])
+    square = settle(units[0])
+    sums1[1].update()
+    square += settle(units[1])
+    sums1[0].spread()
+    mark = len(net.made) - 2 * (cols - 1)
+    square += settle(units[2])
+    square += settle(units[3])
     norm1 = Norm(1)
-    norm1.over_cols(square)
-    sums1.update()
-    norm1.over_rows()
-    sums1.spread()
+    norm1.pair(square)
+    sums1[1].spread()
+    norm1.wide()
+    net.finish(mark)
     rate1 = norm1.rate()
     for part in (0, 1):
         for b in (0, 1):
             field_out[part, :, b * LANES:(b + 1) * LANES] = base[part, b] - rate1 * gtile[part, b]
-    sums1.swap()
-    sums1.done()
+    sums1[0].swap()
+    sums1[0].done()
+
+    def natural(i, parity):
+        begin = parity * LANES
+        spread = jnp.concatenate([right[5, j * width + begin:j * width + begin + LANES, :] for j in range(3)], axis=0)
+        return dot(jnp.concatenate(split3(new_coeffs[1, parity, i]), axis=1), spread)
+
     for i in range(3):
+        acc[i] = natural(i, 0)
+    sums1[1].swap()
+    sums1[1].done()
+    for i in range(3):
+        full = acc[i] + natural(i, 1)
         for b in (0, 1):
             span = slice(b * LANES, (b + 1) * LANES)
             for parity in (0, 1):
-                woven[i, b, pl.ds(parity, half, stride=2), :] = new_coeffs[1, i, parity * half:(parity + 1) * half, span]
+                woven[i, b, pl.ds(parity, half, stride=2), :] = full[parity * half:(parity + 1) * half, span]
             coeffs_out[i, :, span] = woven[i, b]
     net.finish()
 
@@ -698,11 +745,11 @@
     rows3 = rows2 // depth if rows2 % (8 * depth) == 0 else rows2
     left, right = dft_halves(width)
     vmem = pl.BlockSpec(memory_space=pltpu.VMEM)
-    hbm = pl.BlockSpec(memory_space=pl.ANY)
+    hbm = pl.BlockSpec(memory_space=pltpu.HBM)
     semaphores = copies_needed(rows, cols)
     extended = (2, size // LANES, size, LANES)
     freq = (count, 2, width, width)
-    return pl.pallas_call(
+    refined = pl.pallas_call(
         refine_kernel,
         out_shape=(
             jax.ShapeDtypeStruct((2, tile, tile), F32),
@@ -720,17 +767,16 @@
             pltpu.VMEM(freq, BF16),
             pltpu.VMEM(freq, BF16),
             pltpu.VMEM((2, width, width), F32),
-            pltpu.VMEM((3, width, width), F32),
-            pltpu.VMEM((count, width, width), F32),
+            pltpu.VMEM((2, 3, width, LANES), F32),
             pltpu.VMEM((count, width, width), F32),
             pltpu.VMEM(left.shape, BF16),
             pltpu.VMEM(right.shape, BF16),
-            pltpu.VMEM((2, 6, width, width), F32),
-            pltpu.VMEM((2, 6, rows1, width), F32),
-            pltpu.VMEM((2, cols - 1, 6, rows2, width), F32),
-            pltpu.VMEM((2, 6, rows2, width), F32),
-            pltpu.VMEM((2, depth - 1, 6, rows3, width), F32),
-            pltpu.VMEM((3, 3, width, width), F32),
+            pltpu.VMEM((2, 2, 6, width, LANES), F32),
+            pltpu.VMEM((2, 2, 6, rows1, LANES), F32),
+            pltpu.VMEM((2, 2, cols - 1, 6, rows2, LANES), F32),
+            pltpu.VMEM((2, 2, 6, rows2, LANES), F32),
+            pltpu.VMEM((2, 2, depth - 1, 6, rows3, LANES), F32),
+            pltpu.VMEM((2, 2, 3, width, LANES), F32),
             pltpu.VMEM((2, 2, 2, size // LANES, half, LANES), F32),
             pltpu.VMEM((2, 2, 2, half, LANES), F32),
             pltpu.VMEM((2, 2, 2, half, LANES), F32),
@@ -742,19 +788,51 @@
             pltpu.VMEM((2, 2, tile, LANES), F32),
             pltpu.VMEM((2, 2, tile, LANES), F32),
             pltpu.VMEM((2, 8, LANES), F32),
-            pltpu.VMEM((2, cols - 1, 8, LANES), F32),
             pltpu.VMEM((2, 8, LANES), F32),
-            pltpu.VMEM((2, rows - 1, 8, LANES), F32),
+            pltpu.VMEM((2, 8, LANES), F32),
+            pltpu.VMEM((2, depth * cols - 1, 8, LANES), F32),
             pltpu.VMEM((3, width // LANES, width, LANES), F32),
+            pltpu.VMEM((3, width, width), F32),
             pltpu.SemaphoreType.DMA((8,)),
             pltpu.SemaphoreType.DMA((semaphores,)),
             pltpu.SemaphoreType.DMA((semaphores,)),
         ],
         compiler_params=pltpu.CompilerParams(
-            collective_id=0, has_side_effects=True, vmem_limit_bytes=58 * 1024 * 1024
+            collective_id=0, has_side_effects=True, vmem_limit_bytes=60 * 1024 * 1024
         ),
         name="refine",
-    )(object_field, probe, coeffs, patterns, offsets, left, right)
+    )(object_field, probe, coeffs, patterns, jnp.swapaxes(offsets, 2, 3), left, right)
+    return close(*refined)
+
+
+def close_kernel(field, coeffs, field_out, coeffs_out, held, sems):
+    planes = [(field.at[i], field_out.at[i]) for i in range(field.shape[0])]
+    planes += [(coeffs.at[i], coeffs_out.at[i]) for i in range(coeffs.shape[0])]
+    copies = [
+        (pltpu.make_async_copy(source, held.at[n], sems.at[0, n]), pltpu.make_async_copy(held.at[n], target, sems.at[1, n]))
+        for n, (source, target) in enumerate(planes)
+    ]
+    for come, _ in copies:
+        come.start()
+    for come, go in copies:
+        come.wait()
+        go.start()
+    for _, go in copies:
+        go.wait()
+
+
+def close(field, coeffs):
+    hbm = pl.BlockSpec(memory_space=pl.ANY)
+    count = field.shape[0] + coeffs.shape[0]
+    return pl.pallas_call(
+        close_kernel,
+        out_shape=tuple(jax.ShapeDtypeStruct(a.shape, a.dtype) for a in (field, coeffs)),
+        in_specs=[hbm] * 2,
+        out_specs=(hbm, hbm),
+        scratch_shapes=[pltpu.VMEM((count,) + field.shape[1:], F32), pltpu.SemaphoreType.DMA((2, count))],
+        compiler_params=pltpu.CompilerParams(vmem_limit_bytes=60 * 1024 * 1024),
+        name="close",
+    )(field, coeffs)
 
 
 def solution(mesh):

time: 106 us -> 99.1 us (0.935)
  local copies, waits for them, and re-layouts: 5.27 us -> 0 us
  Pallas kernels: 100 us -> 98 us
    unnamed x3 -> x0, local copies, waits for them, and re-layouts: 5.27 us -> none
    pallas_call x1, Pallas kernels: 100 us -> 95.9 us  [local(): pl.pallas_call(refine_kernel, out_shape=(jax.ShapeDtypeStruct((2, tile, t...]
    pallas_call x0 -> x1, Pallas kernels: none -> 2.08 us  [close(): pl.pallas_call(close_kernel, out_shape=tuple((jax.ShapeDtypeStruct(a.shap...]
where the time goes in v2:
time: 99.1 us; the launch traced here: 98.8 us
  Pallas kernels  98 us (99%)
    pallas_call x1, Pallas kernels, local(): pl.pallas_call(refine_kernel, out_shape=(jax.ShapeDtypeStruct((2, tile, t...  95.9 us
    pallas_call x1, Pallas kernels, close(): pl.pallas_call(close_kernel, out_shape=tuple((jax.ShapeDtypeStruct(a.shap...  2.08 us

profile of v2, /device:TPU:0, one launch (start us, length us, event | category | flops | bytes accessed | tf_op | source)
XLA Modules:
  0.0 98.8 jit_solution(8211102094743686752)
XLA Ops:
  0.6 95.9 %refine.1 = (f32[2,256,256]{2,1,0:T(8,128)}, f32[3,256,256]{2,1,0:T(8,128)}) custom-call(f32[2,256,256]{2,1,0:T(8,128)} %field_hbm.1, f32[2,256,256]{2,1,0:T(8,128)} %probe_hbm.1, f32[3,256,256]{2,1,0:T(8,128)} %coeffs_hbm.1, f32[1,1,4,256,256]{4,3,2,1,0:T(8,128)} %pats_hbm.1, s32[1,1,2,4]{3,2,1,0:T(2,128)} %bitcast.1, ...), custom_call_target="tpu_custom_call" | custom-call | tf_op jit(solution)/shard_map/refine/pallas_call | solution.py:752
  96.5 2.1 %close.1 = (f32[2,256,256]{2,1,0:T(8,128)}, f32[3,256,256]{2,1,0:T(8,128)}) custom-call(f32[2,256,256]{2,1,0:T(8,128)} %get-tuple-element.4.field, f32[3,256,256]{2,1,0:T(8,128)} %get-tuple-element.5.coeffs), custom_call_target="tpu_custom_call" | custom-call | tf_op jit(solution)/shard_map/close/pallas_call | solution.py:827

commit v3 on v2

--- a/solution.py
+++ b/solution.py
@@ -64,11 +64,6 @@
     return dot(matrix, jnp.concatenate([high, low, high], axis=0))
 
 
-def from_right(full, matrix):
-    high, low = split(full)
-    return dot(jnp.concatenate([high, low, high], axis=1), matrix)
-
-
 class Copies:
     def __init__(self, send, recv):
         self.send, self.recv, self.used, self.made, self.ended = send, recv, 0, [], 0
@@ -333,7 +328,7 @@
         block = lax.div(ox, LANES)
         return oy, block, ox - block * LANES
 
-    def forward(source, into):
+    def forward(source):
         def visit(p, carry):
             oy, block, shift = place(p)
             window = []
@@ -359,8 +354,16 @@
             im = jnp.concatenate([bands[0][half:], bands[1][half:]], axis=0)
             plus = jnp.concatenate([re[:, :half] + re[:, half:], im[:, :half] + im[:, half:]], axis=1)
             minus = jnp.concatenate([re[:, :half] - re[:, half:], im[:, :half] - im[:, half:]], axis=1)
-            into[p, 0] = from_right(plus, right[0])
-            into[p, 1] = from_right(minus, right[1])
+            for parity, full in ((0, plus), (1, minus)):
+                highs[p, parity], lows[p, parity] = split(full)
+            return carry
+
+        lax.fori_loop(0, count, visit, 0, unroll=True)
+
+    def finish_forward(parity, into):
+        def visit(p, carry):
+            high, low = highs[p, parity], lows[p, parity]
+            into[p, parity] = dot(jnp.concatenate([high, low, high], axis=1), right[parity])
             return carry
 
         lax.fori_loop(0, count, visit, 0, unroll=True)
@@ -544,15 +547,17 @@
 
     block_x, block_g = 2 * (1 - odd_c), 2 * odd_c
 
-    forward(ext, psi)
+    forward(ext)
     sums0 = [Sums(0, parity, coeffs) for parity in (0, 1)]
+    finish_forward(0, psi)
     detect(0, 0, coeffs, None)
     sums0[0].pair()
+    finish_forward(1, psi)
     detect(0, 1, coeffs, None)
     sums0[1].pair()
     sums0[0].over_cols()
+    backward()
     sums0[1].over_cols()
-    backward()
     gather(0, 0, half)
     gather(0, top, half)
     made = fold_rows(0)
@@ -593,20 +598,23 @@
             row=side_dev[which], sends=side_has[which], gets=side_has[which],
         ).start())
 
-    for unit in units:
+    add_fold(0, made, *units[0])
+    push(mids[units[0]])
+    sums0[0].over_z()
+    add_fold(0, made, *units[1])
+    push(mids[units[1]])
+    hand_on(mids[units[0]])
+    for unit in units[2:]:
         add_fold(0, made, *unit)
         push(mids[unit])
-    sums0[0].over_z()
-    hand_on(mids[units[0]])
-    hand_on(mids[units[1]])
+    sums0[0].update()
     sums0[1].over_z()
-    hand_on(mids[units[2]])
-    sums0[0].update()
-    hand_on(mids[units[3]])
+    for unit in units[1:]:
+        hand_on(mids[unit])
     take(units[0])
+    sums0[0].spread()
     sums0[1].update()
     take(units[1])
-    sums0[0].spread()
     take(units[2])
     sums0[1].spread()
     take(units[3])
@@ -624,21 +632,23 @@
         copy.arrived()
     norm0.wide()
 
-    forward(gext, phi)
+    sums0[0].swap()
+    forward(gext)
+    sums0[1].swap()
+    finish_forward(0, phi)
     net.finish(mark)
-    sums0[0].swap()
     rate0 = norm0.rate()
     sums0[0].done()
     sums1 = [Sums(1, parity, new_coeffs.at[0]) for parity in (0, 1)]
     detect(1, 0, new_coeffs.at[0], rate0)
-    sums0[1].swap()
     sums1[0].pair()
+    finish_forward(1, phi)
     sums0[1].done()
     detect(1, 1, new_coeffs.at[0], rate0)
     sums1[1].pair()
     sums1[0].over_cols()
+    backward()
     sums1[1].over_cols()
-    backward()
     gather(1, 0, half)
     gather(1, top, half)
     made = fold_rows(1)
@@ -685,33 +695,32 @@
         add_fold(1, made, *unit)
         push(lasts[unit])
     sums1[0].over_z()
-    hand_on(lasts[units[0]])
     add_fold(1, made, *units[2])
     push(lasts[units[2]])
+    hand_on(lasts[units[0]])
     hand_on(lasts[units[1]])
+    sums1[0].update()
     add_fold(1, made, *units[3])
     push(lasts[units[3]])
     sums1[1].over_z()
     hand_on(lasts[units[2]])
-    sums1[0].update()
+    mark = len(net.made)
+    sums1[0].spread()
     hand_on(lasts[units[3]])
-    square = settle(units[0])
     sums1[1].update()
-    square += settle(units[1])
-    sums1[0].spread()
-    mark = len(net.made) - 2 * (cols - 1)
-    square += settle(units[2])
-    square += settle(units[3])
+    square = 0.0
+    for unit in units:
+        square += settle(unit)
     norm1 = Norm(1)
     norm1.pair(square)
     sums1[1].spread()
     norm1.wide()
+    sums1[0].swap()
     net.finish(mark)
     rate1 = norm1.rate()
     for part in (0, 1):
         for b in (0, 1):
             field_out[part, :, b * LANES:(b + 1) * LANES] = base[part, b] - rate1 * gtile[part, b]
-    sums1[0].swap()
     sums1[0].done()
 
     def natural(i, parity):

time: 99.1 us -> 97.8 us (0.987)
  Pallas kernels: 98 us -> 96.8 us
    pallas_call x1, Pallas kernels: 95.9 us -> 94.7 us  [local(): pl.pallas_call(refine_kernel, out_shape=(jax.ShapeDtypeStruct((2, tile, t...]
where the time goes in v3:
time: 97.8 us; the launch traced here: 97.6 us
  Pallas kernels  96.8 us (99%)
    pallas_call x1, Pallas kernels, local(): pl.pallas_call(refine_kernel, out_shape=(jax.ShapeDtypeStruct((2, tile, t...  94.7 us
    pallas_call x1, Pallas kernels, close(): pl.pallas_call(close_kernel, out_shape=tuple((jax.ShapeDtypeStruct(a.shap...  2.08 us

profile of v3, /device:TPU:0, one launch (start us, length us, event | category | flops | bytes accessed | tf_op | source)
XLA Modules:
  0.0 97.6 jit_solution(1869341999259896952)
XLA Ops:
  0.6 94.7 %refine.1 = (f32[2,256,256]{2,1,0:T(8,128)}, f32[3,256,256]{2,1,0:T(8,128)}) custom-call(f32[2,256,256]{2,1,0:T(8,128)} %field_hbm.1, f32[2,256,256]{2,1,0:T(8,128)} %probe_hbm.1, f32[3,256,256]{2,1,0:T(8,128)} %coeffs_hbm.1, f32[1,1,4,256,256]{4,3,2,1,0:T(8,128)} %pats_hbm.1, s32[1,1,2,4]{3,2,1,0:T(2,128)} %bitcast.1, ...), custom_call_target="tpu_custom_call" | custom-call | tf_op jit(solution)/shard_map/refine/pallas_call | solution.py:761
  95.4 2.1 %close.1 = (f32[2,256,256]{2,1,0:T(8,128)}, f32[3,256,256]{2,1,0:T(8,128)}) custom-call(f32[2,256,256]{2,1,0:T(8,128)} %get-tuple-element.4.field, f32[3,256,256]{2,1,0:T(8,128)} %get-tuple-element.5.coeffs), custom_call_target="tpu_custom_call" | custom-call | tf_op jit(solution)/shard_map/close/pallas_call | solution.py:836

commit v4 on v3

--- a/solution.py
+++ b/solution.py
@@ -158,11 +158,12 @@
     def greet(row, col):
         pl.semaphore_signal(barrier, inc=1, device_id=(row, col), device_id_type=pl.DeviceIdType.MESH)
 
-    for dz, dc in others:
+    near = [(0, dc) for dc in range(1, cols)] + [(dz, 0) for dz in range(1, depth)]
+    when(has_z, lambda: greet(beyond, c))
+    greet(partner, c)
+    for dz, dc in near:
         greet(*chip(dz, dc))
-    greet(partner, c)
-    when(has_z, lambda: greet(beyond, c))
-    greeted = len(others) + 1 + has_z.astype(jnp.int32)
+    greeted = len(near) + 1 + has_z.astype(jnp.int32)
 
     inner = pl.ds(half, tile)
     loads = []

time: 97.8 us -> 96.5 us (0.987)
  Pallas kernels: 96.8 us -> 95.3 us
    pallas_call x1, Pallas kernels: 94.7 us -> 93.3 us  [local(): pl.pallas_call(refine_kernel, out_shape=(jax.ShapeDtypeStruct((2, tile, t...]
where the time goes in v4:
time: 96.5 us; the launch traced here: 96.1 us
  Pallas kernels  95.3 us (99%)
    pallas_call x1, Pallas kernels, local(): pl.pallas_call(refine_kernel, out_shape=(jax.ShapeDtypeStruct((2, tile, t...  93.3 us
    pallas_call x1, Pallas kernels, close(): pl.pallas_call(close_kernel, out_shape=tuple((jax.ShapeDtypeStruct(a.shap...  2.08 us

profile of v4, /device:TPU:0, one launch (start us, length us, event | category | flops | bytes accessed | tf_op | source)
XLA Modules:
  0.0 96.1 jit_solution(5656732411568969557)
XLA Ops:
  0.6 93.3 %refine.1 = (f32[2,256,256]{2,1,0:T(8,128)}, f32[3,256,256]{2,1,0:T(8,128)}) custom-call(f32[2,256,256]{2,1,0:T(8,128)} %field_hbm.1, f32[2,256,256]{2,1,0:T(8,128)} %probe_hbm.1, f32[3,256,256]{2,1,0:T(8,128)} %coeffs_hbm.1, f32[1,1,4,256,256]{4,3,2,1,0:T(8,128)} %pats_hbm.1, s32[1,1,2,4]{3,2,1,0:T(2,128)} %bitcast.1, ...), custom_call_target="tpu_custom_call" | custom-call | tf_op jit(solution)/shard_map/refine/pallas_call | solution.py:762
  93.9 2.1 %close.1 = (f32[2,256,256]{2,1,0:T(8,128)}, f32[3,256,256]{2,1,0:T(8,128)}) custom-call(f32[2,256,256]{2,1,0:T(8,128)} %get-tuple-element.4.field, f32[3,256,256]{2,1,0:T(8,128)} %get-tuple-element.5.coeffs), custom_call_target="tpu_custom_call" | custom-call | tf_op jit(solution)/shard_map/close/pallas_call | solution.py:837

commit v5 on v4

--- a/solution.py
+++ b/solution.py
@@ -203,7 +203,6 @@
                     pads[p, part, b, pl.ds(start, width), :] = jnp.zeros((width, LANES), F32)
         return carry
 
-    lax.fori_loop(0, count, clear, 0)
     for copy in field_loads:
         copy.wait()
     pl.semaphore_wait(barrier, greeted)
@@ -279,6 +278,7 @@
         side[unit][2].start()
     for unit in first_units[:3]:
         straight(unit)
+    lax.fori_loop(0, count, clear, 0)
 
     def reorder(full):
         part = dot(jnp.concatenate(split3(full), axis=1), right[4])
@@ -531,6 +531,7 @@
     def fold_rows(turn):
         made = {}
         for which in (1, 0):
+            gather(turn, pl.multiple_of(edge_row(which), 8), half)
             for part in (0, 1):
                 made[(which, part)] = net.make(
                     grads.at[turn, part, :, at(edge_row(which), half), :], folds.at[turn, which, part],
@@ -559,8 +560,6 @@
     sums0[0].over_cols()
     backward()
     sums0[1].over_cols()
-    gather(0, 0, half)
-    gather(0, top, half)
     made = fold_rows(0)
     gather(0, half, tile)
 
@@ -650,8 +649,6 @@
     sums1[0].over_cols()
     backward()
     sums1[1].over_cols()
-    gather(1, 0, half)
-    gather(1, top, half)
     made = fold_rows(1)
     gather(1, half, tile)
 

time: 96.5 us -> 96.4 us (level)
  no operation moved by 1% of the time
where the time goes in v5:
time: 96.4 us; the launch traced here: 96.1 us
  Pallas kernels  95.3 us (99%)
    pallas_call x1, Pallas kernels, local(): pl.pallas_call(refine_kernel, out_shape=(jax.ShapeDtypeStruct((2, tile, t...  93.2 us
    pallas_call x1, Pallas kernels, close(): pl.pallas_call(close_kernel, out_shape=tuple((jax.ShapeDtypeStruct(a.shap...  2.08 us

profile of v5, /device:TPU:0, one launch (start us, length us, event | category | flops | bytes accessed | tf_op | source)
XLA Modules:
  0.0 96.1 jit_solution(10847229845831658407)
XLA Ops:
  0.6 93.2 %refine.1 = (f32[2,256,256]{2,1,0:T(8,128)}, f32[3,256,256]{2,1,0:T(8,128)}) custom-call(f32[2,256,256]{2,1,0:T(8,128)} %field_hbm.1, f32[2,256,256]{2,1,0:T(8,128)} %probe_hbm.1, f32[3,256,256]{2,1,0:T(8,128)} %coeffs_hbm.1, f32[1,1,4,256,256]{4,3,2,1,0:T(8,128)} %pats_hbm.1, s32[1,1,2,4]{3,2,1,0:T(2,128)} %bitcast.1, ...), custom_call_target="tpu_custom_call" | custom-call | tf_op jit(solution)/shard_map/refine/pallas_call | solution.py:759
  93.8 2.1 %close.1 = (f32[2,256,256]{2,1,0:T(8,128)}, f32[3,256,256]{2,1,0:T(8,128)}) custom-call(f32[2,256,256]{2,1,0:T(8,128)} %get-tuple-element.4.field, f32[3,256,256]{2,1,0:T(8,128)} %get-tuple-element.5.coeffs), custom_call_target="tpu_custom_call" | custom-call | tf_op jit(solution)/shard_map/close/pallas_call | solution.py:834
